TPU v7x, 32 devices: a whole 2x2x4 slice. The times are simulated.
32 devices in a mesh: ctx: 8 (over z, x), tp: 4 (over y, core).
Axes of the slice: x: 2, y: 2, z: 4, core: 2. Of those that a mesh axis runs over, the one named last changes fastest.
Arguments:
- queries: bfloat16 [1024, 4096], P('ctx', 'tp'), may hold values from -160 to 160
- key_rows: bfloat16 [1024, 512], P('ctx', 'tp'), may hold values from -4.5 to 4.5
- value_rows: bfloat16 [1024, 512], P('ctx', 'tp'), may hold values from -6 to 6
- doc_lengths: int32 [4], replicated, may hold values from 1 to 576, 1024 in all
- gate_input: bfloat16 [1024, 4096], P('ctx', 'tp'), may hold values from -6 to 6
- bc_input: bfloat16 [1024, 2, 2, 256], P('ctx'), may hold values from -1.796875 to 1.796875
- step_size: float32 [1024, 64], P('ctx', 'tp'), may hold values from 0.5 to 2
- decay_rate: float32 [64], P('tp'), may hold values from 0 to 1, as said below
- skip_gain: float32 [64], P('tp'), may hold values from 1 to 4
- conv_x: float32 [4, 4096], P(None, 'tp'), may hold values from -3 to 3
- conv_bc: float32 [4, 2, 2, 256], replicated, may hold values from -3 to 3
- norm_gain: float32 [4096], P('tp'), may hold values from 0.1 to 1.9
Outputs:
- mixed: bfloat16 [1024, 4096], P('ctx', 'tp')
Inputs may be any that keep to these rules, and one draw needn't show every extreme that they name: `doc_lengths`: documents lie end to end in token order; the longest has exactly 576 tokens. `decay_rate`: positive rates.
All inputs are finite; a program needn't handle non-finite values.
Results may differ from a plain program's by a relative error of at most 0.02.
Values may be sent and summed in bfloat16 or wider, within the bound.
A program may use at most 128 MiB of HBM per device.

v0:
```python
import math

import jax
import jax.numpy as jnp
from jax import lax
from jax.sharding import PartitionSpec as P

EPSILON = 1e-05
NEGATIVE_FILL = -1e30


def from_behind(x, axis, by):
    size = lax.axis_size(axis)
    pairs = [(i, i + by) for i in range(size) if 0 <= i + by < size]
    return lax.ppermute(x, axis, pairs)


def prefix(x, axis, combine, identity):
    size, mine = (lax.axis_size(axis), lax.axis_index(axis))
    everything = jax.tree.map(
        lambda part, kind: lax.all_gather(part.astype(kind), axis), x, (jnp.bfloat16, jnp.bfloat16)
    )
    start = jax.tree.map(
        lambda part, zero: jnp.broadcast_to(jnp.asarray(zero, part.dtype), part.shape), x, identity
    )

    def step(k, before):
        reached = k < mine
        new = combine(
            before, jax.tree.map(lambda part, own: part[k].astype(own.dtype), everything, x)
        )
        return jax.tree.map(lambda a, b: jnp.where(reached, a, b), new, before)

    return lax.fori_loop(0, size, step, start)


def swapped(block, axis, bit):
    count = lax.axis_size(axis)
    route = []
    for low in range(count):
        high = low | 1 << bit
        if high != low and high < count:
            route += [(low, high), (high, low)]
    return lax.ppermute(block, axis, route)


def first_positions(doc_lengths, positions):
    doc_ends = jnp.cumsum(doc_lengths)
    doc_starts = doc_ends - doc_lengths
    covered = doc_starts[None, :] <= positions[:, None]
    return jnp.max(
        jnp.where(covered, doc_starts[None, :], jnp.zeros_like(doc_starts)[None, :]), axis=1
    )


def attend(
    running, key_block, value_block, key_start, query_rows, query_pos, query_first, score_scale
):
    maximum, totals, summed = running
    key_pos = key_start + jnp.arange(key_block.shape[0], dtype=jnp.int32)
    scores = (
        jnp.einsum("qhd,kd->hqk", query_rows, key_block, preferred_element_type=jnp.float32)
        * score_scale
    )
    visible = (
        (key_pos[None, :] <= query_pos[:, None]) & (key_pos[None, :] >= query_first[:, None])
    )[None]
    masked = jnp.where(visible, scores, NEGATIVE_FILL)
    new_maximum = jnp.maximum(maximum, jnp.max(masked, axis=-1))
    exponent = jnp.where(visible, jnp.exp(masked - new_maximum[..., None]), 0.0)
    factor = jnp.exp(maximum - new_maximum)
    totals = totals * factor + jnp.sum(exponent, axis=-1)
    weights = exponent.astype(jnp.bfloat16)
    summed = summed * factor[..., None] + jnp.einsum(
        "hqk,kd->hqd", weights, value_block, preferred_element_type=jnp.float32
    )
    return (new_maximum, totals, summed)


def key_folder(query_rows, query_pos, query_first, score_scale):
    query_last = jnp.max(query_pos)
    earliest = jnp.min(query_first)

    def maybe_attend(running, key_slab, value_slab, key_start):
        needed = (key_start <= query_last) & (key_start + key_slab.shape[0] > earliest)

        def compute(inner_run):
            return attend(
                inner_run,
                key_slab,
                value_slab,
                key_start,
                query_rows,
                query_pos,
                query_first,
                score_scale,
            )

        def keep(inner_run):
            return inner_run

        return lax.cond(needed, compute, keep, running)

    def fold_keys(running, pieces, offset):
        key_block, value_block = pieces
        key_count = key_block.shape[0]
        block_width = 256
        block_count = key_count // block_width

        def visit(inner_run, entries):
            block_index, key_slab, value_slab = entries
            return (maybe_attend(inner_run, key_slab, value_slab, block_index * block_width), None)

        running, _ = lax.scan(
            visit,
            running,
            (
                jnp.arange(block_count, dtype=jnp.int32),
                key_block.reshape(block_count, block_width, -1),
                value_block.reshape(block_count, block_width, -1),
            ),
        )
        return running

    return fold_keys


def finish(running, row_count):
    maximum, totals, summed = running
    output = summed / totals[..., None]
    return jnp.transpose(output, (1, 0, 2)).reshape(row_count, -1).astype(jnp.bfloat16)


def causal_local(extended, taps, positions, first_token, tap_count):
    row_count = positions.shape[0]
    accumulated = jnp.zeros((row_count,) + extended.shape[1:], jnp.float32)
    for shift_by in range(tap_count):
        tap_rows = extended[tap_count - 1 - shift_by : tap_count - 1 - shift_by + row_count].astype(
            jnp.float32
        )
        usable = (positions - shift_by >= first_token).reshape(
            (row_count,) + (1,) * (extended.ndim - 1)
        )
        accumulated = accumulated + jnp.where(
            usable, tap_rows * taps[tap_count - 1 - shift_by], 0.0
        )
    return accumulated


def combine_states(earlier, following):
    return (earlier[0] * following[0], earlier[1] * following[0][:, None, None] + following[1])


def on_device(
    queries,
    key_rows,
    value_rows,
    doc_lengths,
    gate_input,
    bc_input,
    step_size,
    decay_rate,
    skip_gain,
    conv_x,
    conv_bc,
    norm_gain,
):
    row_count = queries.shape[0]
    head_size = key_rows.shape[1]
    head_count = queries.shape[1] // head_size
    score_scale = 1.0 / math.sqrt(head_size)
    ctx_index = lax.axis_index("ctx")
    block_start = ctx_index * row_count
    own_pos = block_start + jnp.arange(row_count, dtype=jnp.int32)
    own_first = first_positions(doc_lengths, own_pos)
    initial = (
        jnp.full((head_count, row_count), NEGATIVE_FILL, jnp.float32),
        jnp.zeros((head_count, row_count), jnp.float32),
        jnp.zeros((head_count, row_count, head_size), jnp.float32),
    )
    query_rows = queries.reshape(row_count, head_count, head_size)
    running = key_folder(query_rows, own_pos, own_first, score_scale)(
        initial,
        (
            lax.all_gather(key_rows, "ctx", axis=0, tiled=True),
            lax.all_gather(value_rows, "ctx", axis=0, tiled=True),
        ),
        jnp.int32(0),
    )
    attended = finish(running, row_count)
    group_index = lax.axis_index("tp") // 2
    bc_local = lax.dynamic_index_in_dim(bc_input, group_index, 2, keepdims=False)
    conv_bc_local = lax.dynamic_index_in_dim(conv_bc, group_index, 2, keepdims=False)
    tap_count = conv_x.shape[0]
    rim_input, rim_bc = from_behind(
        (attended[row_count - tap_count + 1 :], bc_local[row_count - tap_count + 1 :]), "ctx", 1
    )
    mixed_input = jax.nn.silu(
        causal_local(
            jnp.concatenate([rim_input, attended], 0), conv_x, own_pos, own_first, tap_count
        )
    ).astype(jnp.bfloat16)
    bc_conv = jax.nn.silu(
        causal_local(
            jnp.concatenate([rim_bc, bc_local], 0), conv_bc_local, own_pos, own_first, tap_count
        )
    ).astype(jnp.bfloat16)
    heads_local = step_size.shape[1]
    input_heads = mixed_input.reshape(row_count, heads_local, -1)
    b_values = bc_conv[:, 0]
    c_values = bc_conv[:, 1]
    highest = lax.Precision.HIGHEST
    log_decay = -decay_rate[None, :] * step_size
    cumulated = jnp.cumsum(log_decay, axis=0)
    gram_matrix = jnp.dot(c_values, b_values.T, preferred_element_type=jnp.float32)
    visible = (own_pos[None, :] >= own_first[:, None]) & (own_pos[None, :] <= own_pos[:, None])
    cum_heads = cumulated.T
    log_gap = jnp.where(visible[None], cum_heads[:, :, None] - cum_heads[:, None, :], -jnp.inf)
    mixing = gram_matrix[None] * jnp.exp(log_gap) * step_size.T[:, None, :]
    input_wide = input_heads.astype(jnp.float32)
    inner_part = jnp.einsum("hts,shp->thp", mixing, input_wide, precision=highest)
    last_start = own_first[-1]
    state_weight = jnp.where(
        (own_pos >= last_start)[:, None], jnp.exp(cumulated[-1][None, :] - cumulated), 0.0
    )
    state_weight = state_weight * step_size
    block_state = jnp.einsum(
        "shp,sn->hpn",
        state_weight[:, :, None] * input_wide,
        b_values.astype(jnp.float32),
        precision=highest,
    )
    carry_decay = jnp.where(last_start < block_start, jnp.exp(cumulated[-1]), 0.0)
    identity = (jnp.ones_like(carry_decay), jnp.zeros_like(block_state))
    _, incoming = prefix((carry_decay, block_state), "ctx", combine_states, identity)
    carry_in = (own_first < block_start).astype(jnp.float32)
    carried_part = jnp.einsum(
        "tn,hpn->thp", c_values.astype(jnp.float32), incoming, precision=highest
    )
    carried_part = carried_part * (jnp.exp(cumulated) * carry_in[:, None])[:, :, None]
    ssm_out = inner_part + carried_part + skip_gain[None, :, None] * input_wide
    gated = ssm_out.reshape(row_count, -1) * jax.nn.silu(gate_input.astype(jnp.float32))
    square_sum = jnp.sum(gated * gated, axis=1)
    partner_sum = swapped(square_sum, "tp", 0)
    mean_square = (square_sum + partner_sum) / (2 * gated.shape[1])
    return (gated * lax.rsqrt(mean_square + EPSILON)[:, None] * norm_gain[None, :]).astype(
        jnp.bfloat16
    )


def solution(mesh):
    return jax.shard_map(
        on_device,
        mesh=mesh,
        in_specs=(
            P("ctx", "tp"),
            P("ctx", "tp"),
            P("ctx", "tp"),
            P(),
            P("ctx", "tp"),
            P("ctx", None, None, None),
            P("ctx", "tp"),
            P("tp"),
            P("tp"),
            P(None, "tp"),
            P(),
            P("tp"),
        ),
        out_specs=P("ctx", "tp"),
        check_vma=False,
    )
```

profile of v0, /device:TPU:0, one launch (start us, length us, event | category | flops | bytes accessed | tf_op | source)
XLA Modules:
  0.0 194.0 jit_solution(2875348143827641835)
XLA Ops:
  7.2 0.8 reduce-window.9
  8.7 1.1 copy.67
  10.0 32.8 %all_gather.16 = bf16[1024,128]{1,0:T(8,128)(2,1)S(1)} all-gather(bf16[128,128]{1,0:T(8,128)(2,1)} %param.19), channel_id=1, replica_groups=mesh['ctx'=8,'tp'=4] {'ctx'}, dimensions={0}, use_global_device_ids=true | all-gather | bytes 294912 | tf_op jit(solution)/shard_map/all_gather | solution.py:185
  42.7 30.9 %all_gather.17 = bf16[1024,128]{1,0:T(8,128)(2,1)S(1)} all-gather(bf16[128,128]{1,0:T(8,128)(2,1)} %param.20), channel_id=1, replica_groups=mesh['ctx'=8,'tp'=4] {'ctx'}, dimensions={0}, use_global_device_ids=true | all-gather | bytes 294912 | tf_op jit(solution)/shard_map/all_gather | solution.py:186
  74.6 11.8 %while.29 = (s32[]{:T(128)}, f32[8,128]{1,0:T(8,128)S(1)}, f32[8,128]{1,0:T(8,128)S(1)}, f32[8,128,128]{2,1,0:T(8,128)S(1)}, s32[4]{0:T(128)S(1)}, /*index=5*/s3...) while((s32[]{:T(128)}, f32[8,128]{1,0:T(8,128)S(1)}, ...), condition=%wide.region_9.10_spmd.clone, body=%wide.region_4.9_spmd.clone.sunk | while | flops 136939904 | bytes 4789099 | solution.py:114
  77.2 1.2 conditional.3
  86.8 3.5 %collective-permute-start = (bf16[3,1024]{0,1:T(8,128)(2,1)S(1)}, bf16[3,1024]{0,1:T(8,128)(2,1)S(1)}, u32[]{:S(2)}, u32[]{:S(2)}) collective-permute-start(bf16[3,1024]{0,1:T(8,128)(2,1)S(1)} %bitcast.103), channel_id=1, source_target_pairs={{0,4},{4,8},{8,12},{12,16},{16,20},{20,24},{24,28},{1,5},{5,9},{9,... | collective-permute-start | bytes 18440 | tf_op jit(solution)/shard_map/ppermute | solution.py:15
  90.7 1.9 collective-permute-start.1
  95.6 1.1 bitcast_multiply_fusion
  96.7 1.4 convolution_convert_fusion
  98.2 20.3 %all-gather.1 = bf16[8,1,16]{2,1,0:T(2,128)(2,1)S(1)} all-gather(bf16[1,1,16]{2,1,0:T(2,128)(2,1)S(1)} %get-tuple-element.394), channel_id=1, replica_groups=mesh['ctx'=8,'tp'=4] {'ctx'}, dimensions={0}, use_global_device_ids=true | all-gather | bytes 288 | tf_op jit(solution)/shard_map/all_gather | solution.py:21
  119.1 1.3 convolution_bitcast_fusion
  120.4 53.0 %all-gather.4.cloned.1.call-done = bf16[128,64,256]{2,1,0:T(8,128)(2,1)} async-done(((bf16[16,64,256]{2,1,0:T(8,128)(2,1)}), bf16[128,64,256]{2,1,0:T(8,128)(2,1)}) %all-gather.4.cloned.1.call-update) | async-done | bytes 4194320 | tf_op jit(solution)/shard_map/all_gather | solution.py:21
  173.4 10.6 %while.30 = (s32[]{:T(128)}, f32[16,64,256]{2,1,0:T(8,128)S(1)}, s32[]{:T(128)}, bf16[8,16]{1,0:T(8,128)(2,1)S(1)}, bf16[8,16,64,256]{3,2,1,0:T(8,128)(2,1)}, /*index=5*/s32[]{:T(128)}, s32[]{:T(128)}) while((s32[]{:T(128)}, f32[16,64,256]{2,1,0:T(8,128)S(1)}, s32[]{:T(128)}, bf16[8,16]{1,0:T(8,128)(2,1)S(1)}, ...), condition=%wide.region_12.13_spmd.clone, body=%wide.region_11.12_spmd.clone.sunk | while | flops 1310740 | bytes 2621705 | solution.py:34
  173.4 1.3 fusion.61
  174.8 1.3 fusion.61
  176.1 1.3 fusion.61
  177.4 1.3 fusion.61
  178.8 1.3 fusion.61
  180.1 1.3 fusion.61
  181.4 1.3 fusion.61
  182.8 1.3 fusion.61
  185.0 1.1 collective-permute-done.2
  186.3 0.9 copy.78
  (94 shorter events, 10.9 us)
Async XLA Ops:
  6.5 83.8 %copy-start = (bf16[128,2,2,256]{3,2,1,0:T(2,128)(2,1)S(1)}, bf16[128,2,2,256]{3,2,1,0:T(2,128)(2,1)}, u32[]{:S(2)}) copy-start(bf16[128,2,2,256]{3,2,1,0:T(2,128)(2,1)} %param.23) | copy-start | bytes 786436
  6.5 166.9 %all-gather.4.cloned.1.call-start = ((), (), s32[]{:S(2)}) async-start(), calls=%async_computation | async-start | bytes 4718592 | tf_op jit(solution)/shard_map/all_gather | solution.py:21
  74.5 19.9 %copy-start.7 = (f32[16]{0:T(128)S(1)}, f32[16]{0:T(128)}, u32[]{:S(2)}) copy-start(f32[16]{0:T(128)} %param.25) | copy-start | bytes 196
  74.6 19.9 %copy-start.2 = (f32[128,16]{0,1:T(8,128)S(1)}, f32[128,16]{0,1:T(8,128)}, u32[]{:S(2)}) copy-start(f32[128,16]{0,1:T(8,128)} %param.24) | copy-start | bytes 24580
  74.6 20.3 %copy-start.3 = (f32[4,1024]{1,0:T(4,128)S(1)}, f32[4,1024]{1,0:T(4,128)}, u32[]{:S(2)}) copy-start(f32[4,1024]{1,0:T(4,128)} %param.27) | copy-start | bytes 49156
  74.6 20.4 %copy-start.5 = (f32[4,2,2,256]{3,2,1,0:T(2,128)S(1)}, f32[4,2,2,256]{3,2,1,0:T(2,128)}, u32[]{:S(2)}) copy-start(f32[4,2,2,256]{3,2,1,0:T(2,128)} %param.28) | copy-start | bytes 49156
  86.4 32.3 %copy-start.1 = (bf16[128,1024]{1,0:T(8,128)(2,1)S(1)}, bf16[128,1024]{1,0:T(8,128)(2,1)}, u32[]{:S(2)}) copy-start(bf16[128,1024]{1,0:T(8,128)(2,1)} %param.22) | copy-start | bytes 786436
  86.8 8.8 %collective-permute-start = (bf16[3,1024]{0,1:T(8,128)(2,1)S(1)}, bf16[3,1024]{0,1:T(8,128)(2,1)S(1)}, u32[]{:S(2)}, u32[]{:S(2)}) collective-permute-start(bf16[3,1024]{0,1:T(8,128)(2,1)S(1)} %bitcast.103), channel_id=1, source_target_pairs={{0,4},{4,8},{8,12},{12,16},{16,20},{20,24},{24,28},{1,5},{5,9},{9,... | collective-permute-start | bytes 18440 | tf_op jit(solution)/shard_map/ppermute | solution.py:15
  90.7 4.7 %collective-permute-start.1 = (bf16[3,2,256]{2,0,1:T(4,128)(2,1)S(1)}, bf16[3,2,256]{2,0,1:T(4,128)(2,1)S(1)}, u32[]{:S(2)}, u32[]{:S(2)}) collective-permute-start(bf16[3,2,256]{2,0,1:T(4,128)(2,1)S(1)} %slice_bitcast_fusion), channel_id=1, source_target_pairs={{0,4},{4,8},{8,12},{12,16},{16,20},{20,24},{24,28},{1,5},{5,9},{9,... | collective-permute-start | bytes 9224 | tf_op jit(solution)/shard_map/ppermute | solution.py:15
  173.4 10.7 %copy-start.6 = (f32[16]{0:T(128)S(1)}, f32[16]{0:T(128)}, u32[]{:S(2)}) copy-start(f32[16]{0:T(128)} %param.26) | copy-start | bytes 196
  173.4 12.7 %copy-start.4 = (f32[1024]{0:T(1024)S(1)}, f32[1024]{0:T(1024)}, u32[]{:S(2)}) copy-start(f32[1024]{0:T(1024)} %param.29) | copy-start | bytes 12292
  184.9 1.2 collective-permute-start.2
Sparse Core Ops, SparseCore 0:
  98.3 75.0 all-gather.3
where the time goes:
time: 195 us; the launch traced here: 194 us
  blocking collectives  84 us (43%)
  waiting for transfers between devices  54.1 us (28%)
  other arithmetic  16.9 us (9%)
  between operations  14.4 us (7%)
  loops' own time  8.25 us (4%)
  local copies, waits for them, and re-layouts  6.67 us (3%)
  starting transfers between devices  5.44 us (3%)
  matrix products  4.25 us (2%)
    all_gather x1, waiting for transfers between devices, prefix(): lax.all_gather(part.astype(kind), axis)  53 us
    all_gather x1, blocking collectives, on_device(): lax.all_gather(key_rows, 'ctx', axis=0, tiled=True)  32.8 us
    all_gather x1, blocking collectives, on_device(): lax.all_gather(value_rows, 'ctx', axis=0, tiled=True)  30.9 us
    all_gather x1, blocking collectives, prefix(): lax.all_gather(part.astype(kind), axis)  20.3 us
    select_n x8, other arithmetic, step(): return jax.tree.map(lambda a, b: jnp.where(reached, a, b), new, before)  10.4 us
    another operation x1, loops' own time, fold_keys(): lax.scan(visit, running, (jnp.arange(block_count, dtype=jnp.int32), key_b...  7.9 us
    ppermute x2, starting transfers between devices, from_behind(): return lax.ppermute(x, axis, pairs)  5.37 us
  transfers between devices with their start and end apart: 4, of which 2 were waited for; matrix products, arithmetic and copies ran while one was open for 2% of the time, Pallas kernels for 0%

commit v1 on v0

--- a/solution.py
+++ b/solution.py
@@ -1,8 +1,11 @@
+import functools
 import math
 
 import jax
 import jax.numpy as jnp
 from jax import lax
+from jax.experimental import pallas as pl
+from jax.experimental.pallas import tpu as pltpu
 from jax.sharding import PartitionSpec as P
 
 EPSILON = 1e-05
@@ -248,9 +251,471 @@
     )
 
 
+LANES = 128
+RIM = 16
+MESH = pl.DeviceIdType.MESH
+
+
+def dot_nt(a, b):
+    return lax.dot_general(a, b, (((1,), (1,)), ((), ())), preferred_element_type=jnp.float32)
+
+
+def dot_tn(a, b):
+    return lax.dot_general(a, b, (((0,), (0,)), ((), ())), preferred_element_type=jnp.float32)
+
+
+def dot_nn(a, b):
+    return jnp.dot(a, b, preferred_element_type=jnp.float32)
+
+
+def silu(v):
+    return v / (1.0 + jnp.exp(-v))
+
+
+def fused_kernel(
+    n,
+    window,
+    doc_ref,
+    rate_ref,
+    skip_ref,
+    q_ref,
+    k_ref,
+    v_ref,
+    gate_ref,
+    bc_ref,
+    dt_ref,
+    taps_ref,
+    bc_taps_ref,
+    gain_ref,
+    out_ref,
+    kv,
+    q_rim,
+    bc_rim,
+    bc_all,
+    x_out,
+    x_all,
+    dt_all,
+    y_out,
+    y_all,
+    gated_ref,
+    sq_own,
+    sq_other,
+    kv_send,
+    kv_recv,
+    rim_send,
+    rim_recv,
+    bc_send,
+    bc_recv,
+    bc_core_send,
+    bc_core_recv,
+    x_send,
+    x_recv,
+    dt_send,
+    dt_recv,
+    y_send,
+    y_recv,
+    sq_sem,
+):
+    rows = q_ref.shape[0]
+    me = lax.axis_index("ctx")
+    tp = lax.axis_index("tp")
+    core = lax.rem(tp, 2)
+    group = tp // 2
+    tp_other = tp + 1 - 2 * core
+    parity = lax.rem(me, 2)
+    pair = me + 1 - 2 * parity
+    state_size = bc_all.shape[3]
+    ndoc = doc_ref.shape[0]
+    groups = bc_ref.shape[1] // (2 * state_size)
+
+    def to_ctx(src, dst, send, recv, where):
+        return pltpu.make_async_remote_copy(
+            src_ref=src, dst_ref=dst, send_sem=send, recv_sem=recv,
+            device_id=(where, tp), device_id_type=MESH)
+
+    def to_core(src, dst, send, recv):
+        return pltpu.make_async_remote_copy(
+            src_ref=src, dst_ref=dst, send_sem=send, recv_sem=recv,
+            device_id=(me, tp_other), device_id_type=MESH)
+
+    barrier = pltpu.get_barrier_semaphore()
+    for k in range(1, n):
+        pl.semaphore_signal(
+            barrier, inc=1, device_id=(lax.rem(me + k, n), tp), device_id_type=MESH)
+    pl.semaphore_signal(barrier, inc=1, device_id=(me, tp_other), device_id_type=MESH)
+    kv[0, 0] = k_ref[...]
+    kv[0, 1] = v_ref[...]
+    for r in range(1, window):
+        @pl.when(me < r)
+        def _():
+            kv[r] = jnp.zeros(kv.shape[1:], kv.dtype)
+
+    @pl.when(me == 0)
+    def _():
+        q_rim[...] = jnp.zeros(q_rim.shape, q_rim.dtype)
+        bc_rim[...] = jnp.zeros(bc_rim.shape, bc_rim.dtype)
+
+    pl.semaphore_wait(barrier, n)
+
+    half = window // 2
+    direct = []
+    for k in range(1, half + 1):
+        copy = to_ctx(kv.at[0], kv.at[2 * k], kv_send.at[k], kv_recv.at[2 * k],
+                      jnp.minimum(me + 2 * k, n - 1))
+        wanted = me + 2 * k < n
+        if 2 * k >= window:
+            wanted = wanted & (parity == 1)
+        direct.append((wanted, copy))
+    even = parity == 0
+    odd = parity == 1
+    relay_even = [to_ctx(kv.at[r], kv.at[r + 1], kv_send.at[half + 1 + r], kv_recv.at[r + 1], pair)
+                  for r in range(0, window, 2)]
+    relay_odd = [to_ctx(kv.at[r], kv.at[r - 1], kv_send.at[half + 1 + r], kv_recv.at[r - 1], pair)
+                 for r in range(2, window + 1, 2)]
+    nxt = jnp.minimum(me + 1, n - 1)
+    rim_q = to_ctx(q_ref.at[pl.ds(rows - RIM, RIM)], q_rim, rim_send.at[0], rim_recv.at[0], nxt)
+    rim_b = to_ctx(bc_ref.at[pl.ds(rows - RIM, RIM)], bc_rim, rim_send.at[1], rim_recv.at[1], nxt)
+
+    @pl.when(me + 1 < n)
+    def _():
+        rim_b.start()
+
+    @pl.when(even)
+    def _():
+        relay_even[0].start()
+
+    for wanted, copy in direct:
+        @pl.when(wanted)
+        def _():
+            copy.start()
+
+    @pl.when(me + 1 < n)
+    def _():
+        rim_q.start()
+
+    for k in range(1, n):
+        d = lax.rem(me + k, n)
+        to_ctx(dt_ref.at[d], dt_all.at[me], dt_send.at[k], dt_recv.at[me], d).start()
+    dt_all[me] = dt_ref[me]
+
+    starts = []
+    total = jnp.int32(0)
+    for i in range(ndoc):
+        starts.append(total)
+        total = total + doc_ref[i]
+
+    def first_of(pos):
+        first = jnp.zeros_like(pos)
+        for s in starts:
+            first = jnp.where(s <= pos, s, first)
+        return first
+
+    row_iota = lax.broadcasted_iota(jnp.int32, (rows, LANES), 0)
+    lane_iota = lax.broadcasted_iota(jnp.int32, (rows, LANES), 1)
+    base = me * rows
+    own_pos = base + row_iota
+    own_first = first_of(own_pos)
+    tap_count = taps_ref.shape[0]
+    since = own_pos - own_first
+
+    def conv(extended, taps, wide):
+        acc = None
+        for m in range(tap_count):
+            part = extended[8 - m: 8 - m + rows] * taps[tap_count - 1 - m: tap_count - m]
+            seen = since >= m
+            if wide > 1:
+                seen = jnp.concatenate([seen.astype(jnp.int32)] * wide, axis=1) > 0
+            part = jnp.where(seen, part, 0.0)
+            acc = part if acc is None else acc + part
+        return silu(acc).astype(jnp.bfloat16)
+
+    @pl.when(me > 0)
+    def _():
+        rim_b.wait_recv()
+
+    for i in range(2):
+        for piece in range(state_size // LANES):
+            cols = pl.ds(pl.multiple_of(
+                (i * groups + group) * state_size + piece * LANES, LANES), LANES)
+            extended = jnp.concatenate(
+                [bc_rim[:, cols].astype(jnp.float32)[RIM - 8:], bc_ref[:, cols].astype(jnp.float32)], axis=0)
+            bc_all[me, i, :, piece * LANES:(piece + 1) * LANES] = conv(extended, bc_taps_ref[:, cols], 1)
+
+    column = [lax.rem(me + 2 * k, n) for k in range(1, n // 2)]
+
+    def relay_bc(s, slot):
+        return to_ctx(bc_all.at[s, core], bc_all.at[s, core], bc_send.at[slot], bc_recv.at[s], pair)
+
+    def share_bc(s, slot):
+        return to_core(bc_all.at[s, core], bc_all.at[s, core], bc_core_send.at[slot], bc_core_recv.at[s])
+
+    bc_own = [to_ctx(bc_all.at[me, core], bc_all.at[me, core], bc_send.at[0], bc_recv.at[me], pair)]
+    for k, d in enumerate(column):
+        bc_own.append(to_ctx(bc_all.at[me, core], bc_all.at[me, core],
+                             bc_send.at[1 + k], bc_recv.at[me], d))
+
+    for r in range(2, window + 1, 2):
+        cond = me >= r
+        if r >= window:
+            cond = cond & odd
+
+        @pl.when(cond)
+        def _():
+            to_ctx(kv.at[0], kv.at[r], kv_send.at[0], kv_recv.at[r], pair).wait_recv()
+
+        if r < window:
+            @pl.when(even & (me >= r))
+            def _():
+                relay_even[r // 2].start()
+
+        @pl.when(odd & (me >= r))
+        def _():
+            relay_odd[r // 2 - 1].start()
+        if r == 2:
+            for copy in bc_own:
+                copy.start()
+    for r in range(1, window, 2):
+        @pl.when(me >= r)
+        def _():
+            to_ctx(kv.at[0], kv.at[r], kv_send.at[0], kv_recv.at[r], pair).wait_recv()
+
+    @pl.when(me > 0)
+    def _():
+        rim_q.wait_recv()
+
+    keys = jnp.concatenate([kv[r, 0] for r in range(window)], axis=0)
+    values = jnp.concatenate([kv[r, 1] for r in range(window)], axis=0)
+    scale = 1.0 / math.sqrt(k_ref.shape[1])
+
+    def bias_of(pos):
+        first = first_of(pos)
+        parts = []
+        for r in range(window):
+            key_pos = (me - r) * rows + lane_iota
+            parts.append(jnp.where((key_pos <= pos) & (key_pos >= first), 0.0, NEGATIVE_FILL))
+        return jnp.concatenate(parts, axis=1)
+
+    def attention(block, bias):
+        scores = dot_nt(block, keys) * scale + bias
+        exponent = jnp.exp(scores - jnp.max(scores, axis=1, keepdims=True))
+        totals = jnp.sum(exponent, axis=1, keepdims=True)
+        summed = dot_nn(exponent.astype(jnp.bfloat16), values)
+        return (summed / totals).astype(jnp.bfloat16).astype(jnp.float32)
+
+    rim_block = jnp.concatenate(
+        [q_rim[:, h * LANES:(h + 1) * LANES] for h in range(n)], axis=0)
+    rim_pos = base - RIM + lax.rem(row_iota, RIM)
+    gated_ref[0] = attention(rim_block, bias_of(rim_pos))
+    bias = bias_of(own_pos)
+
+    def recv_bc(s):
+        to_ctx(bc_all.at[s, core], bc_all.at[s, core], bc_send.at[0], bc_recv.at[s], pair).wait_recv()
+
+    for k in range(n):
+        h = lax.rem(me + 1 + k, n)
+        cols = pl.ds(pl.multiple_of(h * LANES, LANES), LANES)
+        attended = attention(q_ref[:, cols], bias)
+        rim = gated_ref[0, pl.ds(pl.multiple_of(h * RIM + RIM - 8, 8), 8), :]
+        x = conv(jnp.concatenate([rim, attended], axis=0), taps_ref[:, cols], 1)
+        if k < n - 1:
+            x_out[h] = x
+            to_ctx(x_out.at[h], x_all.at[me], x_send.at[k], x_recv.at[me], h).start()
+        else:
+            x_all[me] = x
+        if k >= n // 2 and k - n // 2 < len(column):
+            s = column[k - n // 2]
+            recv_bc(s)
+            relay_bc(s, n // 2 + k - n // 2).start()
+            share_bc(s, k - n // 2).start()
+    crossed = [pair] + [lax.rem(pair + 2 * k, n) for k in range(1, n // 2)]
+    for k, s in enumerate(crossed):
+        recv_bc(s)
+        share_bc(s, n // 2 - 1 + k).start()
+
+    upper = (row_iota <= lane_iota).astype(jnp.float32)
+    left = lane_iota < LANES // 2
+    rate = [rate_ref[2 * me + a] for a in range(2)]
+    skip = jnp.where(left[:1], skip_ref[2 * me], skip_ref[2 * me + 1])
+    for k in range(1, n):
+        s = lax.rem(me + k, n)
+        to_ctx(dt_ref.at[s], dt_all.at[s], dt_send.at[k], dt_recv.at[s], s).wait_recv()
+    dt_rows = [jnp.concatenate([dt_all[i, a:a + 1] for i in range(n)], axis=0) for a in range(2)]
+    cum_rows = [jnp.dot(-rate[a] * dt_rows[a], upper, precision=lax.Precision.HIGHEST,
+                        preferred_element_type=jnp.float32) for a in range(2)]
+    state = jnp.zeros((state_size, LANES), jnp.float32)
+    for i in range(n):
+        @pl.when(me != i)
+        def _():
+            to_ctx(x_all.at[i], x_all.at[i], x_send.at[0], x_recv.at[i], pair).wait_recv()
+            other = 1 - core
+            to_core(bc_all.at[i, other], bc_all.at[i, other], bc_core_send.at[0],
+                    bc_core_recv.at[i]).wait_recv()
+
+        x = x_all[i]
+        b, c = bc_all[i, 0], bc_all[i, 1]
+        xw = x.astype(jnp.float32)
+        start = i * rows
+        pos = start + row_iota
+        first = first_of(pos)
+        key_pos = start + lane_iota
+        visible = (key_pos >= first) & (key_pos <= pos)
+        cum = [cum_rows[a][i:i + 1] for a in range(2)]
+        dts = [dt_rows[a][i:i + 1] for a in range(2)]
+        side = (rows // 2, LANES)
+        cum_col = jnp.concatenate([jnp.broadcast_to(r, side) for r in cum], axis=0).T
+        dt_col = jnp.concatenate([jnp.broadcast_to(r, side) for r in dts], axis=0).T
+        gram = jnp.where(visible, dot_nt(c, b), 0.0)
+        mix = []
+        for a in range(2):
+            col = cum_col[:, a * (LANES // 2):a * (LANES // 2) + 1]
+            gap = jnp.where(visible, col - cum[a], 0.0)
+            mix.append((gram * jnp.exp(gap) * dts[a]).astype(jnp.bfloat16))
+        both = jnp.concatenate([jnp.where(left, xw, 0.0), jnp.where(left, 0.0, xw)], axis=0)
+        y = dot_nn(jnp.concatenate(mix, axis=1), both.astype(jnp.bfloat16)) + skip * xw
+        if i > 0:
+            carried = dot_nn(c, state.astype(jnp.bfloat16))
+            y = y + jnp.where(first < start, jnp.exp(cum_col), 0.0) * carried
+        if i < n - 1:
+            last_start = first[rows - 1:rows]
+            cum_last = cum_col[rows - 1:rows]
+            weight = jnp.where(pos >= last_start, jnp.exp(cum_last - cum_col) * dt_col, 0.0)
+            grown = dot_tn(b, (xw * weight).astype(jnp.bfloat16))
+            keep = jnp.where(last_start < start, jnp.exp(cum_last), 0.0)
+            state = keep * state + grown
+        y = y.astype(jnp.bfloat16)
+
+        @pl.when(me != i)
+        def _():
+            y_out[i] = y
+            to_ctx(y_out.at[i], y_all.at[me], y_send.at[i], y_recv.at[me], i).start()
+
+        @pl.when(me == i)
+        def _():
+            y_all[me] = y
+
+    squares = jnp.zeros((rows, LANES), jnp.float32)
+    for h in range(n):
+        @pl.when(me != h)
+        def _():
+            to_ctx(y_out.at[h], y_all.at[h], y_send.at[h], y_recv.at[h], pair).wait_recv()
+
+        z = gate_ref[:, h * LANES:(h + 1) * LANES].astype(jnp.float32)
+        gated = y_all[h].astype(jnp.float32) * silu(z)
+        gated_ref[h] = gated
+        squares = squares + gated * gated
+    sq_own[...] = squares
+    swap = to_core(sq_own, sq_other, sq_sem.at[0], sq_sem.at[1])
+    swap.start()
+
+    for wanted, copy in direct:
+        @pl.when(wanted)
+        def _():
+            copy.wait_send()
+    for j, r in enumerate(range(0, window, 2)):
+        @pl.when(even & (me >= r))
+        def _():
+            relay_even[j].wait_send()
+    for j, r in enumerate(range(2, window + 1, 2)):
+        @pl.when(odd & (me >= r))
+        def _():
+            relay_odd[j].wait_send()
+
+    @pl.when(me + 1 < n)
+    def _():
+        rim_q.wait_send()
+        rim_b.wait_send()
+    for copy in bc_own:
+        copy.wait_send()
+    for k, s in enumerate(column):
+        relay_bc(s, n // 2 + k).wait_send()
+        share_bc(s, k).wait_send()
+    for k, s in enumerate(crossed):
+        share_bc(s, n // 2 - 1 + k).wait_send()
+    for k in range(n - 1):
+        h = lax.rem(me + 1 + k, n)
+        to_ctx(x_out.at[h], x_all.at[me], x_send.at[k], x_recv.at[me], h).wait_send()
+        to_ctx(dt_ref.at[h], dt_all.at[me], dt_send.at[k + 1], dt_recv.at[me], h).wait_send()
+    for i in range(n):
+        @pl.when(me != i)
+        def _():
+            to_ctx(y_out.at[i], y_all.at[me], y_send.at[i], y_recv.at[me], i).wait_send()
+    swap.wait()
+    width = 2 * n * LANES
+    mean_square = jnp.sum(sq_own[...] + sq_other[...], axis=1, keepdims=True) / width
+    factor = lax.rsqrt(mean_square + EPSILON)
+    for h in range(n):
+        cols = slice(h * LANES, (h + 1) * LANES)
+        out_ref[:, cols] = (gated_ref[h] * factor * gain_ref[:, cols]).astype(jnp.bfloat16)
+
+
+def fused_on_device(
+    queries, key_rows, value_rows, doc_lengths, gate_input, bc_input, step_size,
+    decay_rate, skip_gain, conv_x, conv_bc, norm_gain,
+):
+    n = lax.axis_size("ctx")
+    rows = queries.shape[0]
+    state_size = bc_input.shape[3]
+    longest = n * rows // 2 + 64
+    window = 1 + -(-(longest - 1) // rows)
+    bc = bc_input.reshape(rows, -1)
+    dt = jnp.pad(step_size.T.reshape(n, 2, rows), ((0, 0), (0, 6), (0, 0)))
+    bf16, f32 = jnp.bfloat16, jnp.float32
+    vmem = pl.BlockSpec(memory_space=pltpu.VMEM)
+    smem = pl.BlockSpec(memory_space=pltpu.SMEM)
+    dma = pltpu.SemaphoreType.DMA
+    half = window // 2
+    return pl.pallas_call(
+        functools.partial(fused_kernel, n, window),
+        out_shape=jax.ShapeDtypeStruct(queries.shape, bf16),
+        in_specs=[smem] * 3 + [vmem] * 9,
+        out_specs=vmem,
+        scratch_shapes=[
+            pltpu.VMEM((window + 1, 2, rows, LANES), bf16),
+            pltpu.VMEM((RIM, queries.shape[1]), bf16),
+            pltpu.VMEM((RIM, bc.shape[1]), bf16),
+            pltpu.VMEM((n, 2, rows, state_size), bf16),
+            pltpu.VMEM((n, rows, LANES), bf16),
+            pltpu.VMEM((n, rows, LANES), bf16),
+            pltpu.VMEM((n, 8, LANES), f32),
+            pltpu.VMEM((n, rows, LANES), bf16),
+            pltpu.VMEM((n, rows, LANES), bf16),
+            pltpu.VMEM((n, rows, LANES), f32),
+            pltpu.VMEM((rows, LANES), f32),
+            pltpu.VMEM((rows, LANES), f32),
+            dma((half + 2 + window,)),
+            dma((window + 1,)),
+            dma((2,)),
+            dma((2,)),
+            dma((n,)),
+            dma((n,)),
+            dma((n,)),
+            dma((n,)),
+            dma((n,)),
+            dma((n,)),
+            dma((n,)),
+            dma((n,)),
+            dma((n,)),
+            dma((n,)),
+            dma((2,)),
+        ],
+        compiler_params=pltpu.CompilerParams(
+            collective_id=0, has_side_effects=True, vmem_limit_bytes=32 * 1024 * 1024),
+    )(
+        doc_lengths, decay_rate, skip_gain, queries, key_rows, value_rows, gate_input, bc, dt,
+        conv_x, conv_bc.reshape(conv_bc.shape[0], -1), norm_gain.reshape(1, -1),
+    )
+
+
+def plan(queries, key_rows, *rest):
+    blocks = queries.shape[1] // LANES
+    if blocks == lax.axis_size("ctx") and queries.shape[0] == LANES:
+        return fused_on_device(queries, key_rows, *rest)
+    return on_device(queries, key_rows, *rest)
+
+
 def solution(mesh):
     return jax.shard_map(
-        on_device,
+        plan,
         mesh=mesh,
         in_specs=(
             P("ctx", "tp"),

time: 195 us -> 41.8 us (0.21)
  blocking collectives: 84 us -> 0 us
  waiting for transfers between devices: 54.1 us -> 0 us
  Pallas kernels: 0 us -> 37.2 us
  other arithmetic: 16.9 us -> 0 us
  between operations: 14.4 us -> 0.13 us
  loops' own time: 8.25 us -> 0 us
  starting transfers between devices: 5.44 us -> 0 us
  matrix products: 4.25 us -> 0 us
  local copies, waits for them, and re-layouts: 6.67 us -> 4.1 us
    all_gather x3 -> x0, blocking collectives: 84 us -> none  [the longest x1 32.8 us: on_device(): lax.all_gather(key_rows, 'ctx', axis=0, tiled=True)]
    all_gather x1 -> x0, waiting for transfers between devices: 53 us -> none  [prefix(): lax.all_gather(part.astype(kind), axis)]
    pallas_call x0 -> x1, Pallas kernels: none -> 37.2 us  [fused_on_device(): pl.pallas_call(functools.partial(fused_kernel, n, window), out_shape=jax....]
    select_n x8 -> x0, other arithmetic: 10.4 us -> none  [step(): return jax.tree.map(lambda a, b: jnp.where(reached, a, b), new, before)]
    another operation x6 -> x0, loops' own time: 8.25 us -> none  [the longest x1 7.9 us: fold_keys(): lax.scan(visit, running, (jnp.arange(block_count, dtype=jnp.int32), key_b...]
    ppermute x3 -> x0, starting transfers between devices: 5.44 us -> none  [the longest x2 5.37 us: from_behind(): return lax.ppermute(x, axis, pairs)]
    dot_general x6 -> x0, matrix products: 4.25 us -> none  [the longest x1 1.39 us: on_device(): jnp.einsum('shp,sn->hpn', state_weight[:, :, None] * input_wide, b_values...]
    dynamic_slice x5 -> x0, local copies, waits for them, and re-layouts: 2.9 us -> none  [the longest x4 2.62 us: fold_keys(): lax.scan(visit, running, (jnp.arange(block_count, dtype=jnp.int32), key_b...]
  transfers between devices with their start and end apart: 4 -> 0, of which waited for: 2 -> 0; matrix products, arithmetic and copies ran while one was open for 2% -> 0% of each run, Pallas kernels for 0% -> 0%
where the time goes in v1:
time: 41.8 us; the launch traced here: 41.4 us
  Pallas kernels  37.2 us (89%)
  local copies, waits for them, and re-layouts  4.1 us (10%)
    pallas_call x1, Pallas kernels, fused_on_device(): pl.pallas_call(functools.partial(fused_kernel, n, window), out_shape=jax....  37.2 us
    unnamed x19, local copies, waits for them, and re-layouts  1.46 us
    reshape x1, local copies, waits for them, and re-layouts, fused_on_device(): bc = bc_input.reshape(rows, -1)  1.18 us

profile of v1, /device:TPU:0, one launch (start us, length us, event | category | flops | bytes accessed | tf_op | source)
XLA Modules:
  0.0 41.4 jit_solution(7284217254260835440)
XLA Ops:
  0.0 0.0 copy-start.3
  0.0 0.7 %reshape.14.bc_taps_ref = f32[4,1024]{1,0:T(4,128)S(1)} reshape(f32[4,2,2,256]{3,2,1,0:T(2,128)} %param.22) | data formatting | bytes 32768 | tf_op jit(solution)/shard_map/reshape | solution.py:705
  0.7 0.0 copy-start.2
  0.8 0.0 copy-start.5
  0.8 0.0 copy-start.6
  0.8 0.0 copy-start.7
  0.8 0.0 copy-start.8
  0.8 0.7 %pad.4.dt_ref = f32[8,8,128]{2,1,0:T(8,128)S(1)} pad(f32[8,2,128]{2,1,0:T(2,128)} %bitcast.5, f32[]{:T(128)} %constant.2.clone.1), padding=0_0x0_6x0_0 | pad | bytes 40964 | tf_op jit(solution)/shard_map/jit(_pad)/pad | solution.py:661
  1.5 0.0 copy-start
  1.5 0.0 copy-start.1
  1.5 1.2 %reshape.12.bc_ref = bf16[128,1024]{1,0:T(8,128)(2,1)S(1)} reshape(bf16[128,2,2,256]{3,2,1,0:T(2,128)(2,1)} %param.17) | data formatting | bytes 524288 | tf_op jit(solution)/shard_map/reshape | solution.py:660
  2.7 0.0 copy-done.3
  2.7 0.0 copy-done.2
  2.7 0.0 copy-done.5
  2.7 0.0 copy-done.6
  2.8 0.0 copy-done.7
  2.8 0.0 copy-done.8
  2.8 0.0 copy-done
  2.8 0.0 copy-done.1
  2.8 0.0 copy-start.4
  2.8 0.7 %copy-done.4 = f32[4,1024]{1,0:T(4,128)S(1)} copy-done((f32[4,1024]{1,0:T(4,128)S(1)}, f32[4,1024]{1,0:T(4,128)}, u32[]{:S(2)}) %copy-start.4) | copy-done | bytes 16408
  3.5 37.2 %shard_map.118 = bf16[128,1024]{1,0:T(8,128)(2,1)S(1)} custom-call(s32[4]{0:T(128)S(1)} %copy-done.6, f32[16]{0:T(128)S(1)} %copy-done.7, f32[16]{0:T(128)S(1)} %copy-done.8, bf16[128,1024]{1,0:T(8,128)(2,1)S(1)} %copy-done, bf16[128,128]{1,0:T(8,128)(2,1)S(1)} %copy-done.2, bf16[128,128]{1,0:T(8,128)(2,1)S(1)} %copy-done.3, ...), custom_call_target="tpu_custom_call" | custom-call | tf_op jit(solution)/shard_map/pallas_call | solution.py:667
  40.7 0.7 %copy.14 = bf16[128,1024]{1,0:T(8,128)(2,1)} copy(bf16[128,1024]{1,0:T(8,128)(2,1)S(1)} %shard_map.118) | data formatting | bytes 524288
Async XLA Ops:
  0.0 2.7 %copy-start.3 = (bf16[128,128]{1,0:T(8,128)(2,1)S(1)}, bf16[128,128]{1,0:T(8,128)(2,1)}, u32[]{:S(2)}) copy-start(bf16[128,128]{1,0:T(8,128)(2,1)} %v_ref.1) | copy-start | bytes 98308
  0.7 2.0 %copy-start.2 = (bf16[128,128]{1,0:T(8,128)(2,1)S(1)}, bf16[128,128]{1,0:T(8,128)(2,1)}, u32[]{:S(2)}) copy-start(bf16[128,128]{1,0:T(8,128)(2,1)} %k_ref.1) | copy-start | bytes 98308
  0.8 2.0 %copy-start.5 = (f32[1024]{0:T(1024)S(1)}, f32[1024]{0:T(1024)}, u32[]{:S(2)}) copy-start(f32[1024]{0:T(1024)} %param.23) | copy-start | bytes 12292
  0.8 2.0 %copy-start.6 = (s32[4]{0:T(128)S(1)}, s32[4]{0:T(128)}, u32[]{:S(2)}) copy-start(s32[4]{0:T(128)} %doc_ref.1) | copy-start | bytes 52
  0.8 2.0 %copy-start.7 = (f32[16]{0:T(128)S(1)}, f32[16]{0:T(128)}, u32[]{:S(2)}) copy-start(f32[16]{0:T(128)} %rate_ref.1) | copy-start | bytes 196
  0.8 2.0 %copy-start.8 = (f32[16]{0:T(128)S(1)}, f32[16]{0:T(128)}, u32[]{:S(2)}) copy-start(f32[16]{0:T(128)} %skip_ref.1) | copy-start | bytes 196
  1.5 1.2 %copy-start = (bf16[128,1024]{1,0:T(8,128)(2,1)S(1)}, bf16[128,1024]{1,0:T(8,128)(2,1)}, u32[]{:S(2)}) copy-start(bf16[128,1024]{1,0:T(8,128)(2,1)} %q_ref.1) | copy-start | bytes 786436
  1.5 1.3 %copy-start.1 = (bf16[128,1024]{1,0:T(8,128)(2,1)S(1)}, bf16[128,1024]{1,0:T(8,128)(2,1)}, u32[]{:S(2)}) copy-start(bf16[128,1024]{1,0:T(8,128)(2,1)} %gate_ref.1) | copy-start | bytes 786436
  2.8 0.7 %copy-start.4 = (f32[4,1024]{1,0:T(4,128)S(1)}, f32[4,1024]{1,0:T(4,128)}, u32[]{:S(2)}) copy-start(f32[4,1024]{1,0:T(4,128)} %taps_ref.1) | copy-start | bytes 49156

commit v2 on v1

--- a/solution.py
+++ b/solution.py
@@ -283,7 +283,7 @@
     v_ref,
     gate_ref,
     bc_ref,
-    dt_ref,
+    step_ref,
     taps_ref,
     bc_taps_ref,
     gain_ref,
@@ -294,7 +294,12 @@
     bc_all,
     x_out,
     x_all,
+    dt_own,
     dt_all,
+    mix_ref,
+    weight_ref,
+    carry_ref,
+    state_ref,
     y_out,
     y_all,
     gated_ref,
@@ -355,6 +360,10 @@
         q_rim[...] = jnp.zeros(q_rim.shape, q_rim.dtype)
         bc_rim[...] = jnp.zeros(bc_rim.shape, bc_rim.dtype)
 
+    steps = step_ref[...]
+    for d in range(n):
+        dt_own[d, 0:2] = steps[2 * d:2 * d + 2]
+
     pl.semaphore_wait(barrier, n)
 
     half = window // 2
@@ -395,8 +404,8 @@
 
     for k in range(1, n):
         d = lax.rem(me + k, n)
-        to_ctx(dt_ref.at[d], dt_all.at[me], dt_send.at[k], dt_recv.at[me], d).start()
-    dt_all[me] = dt_ref[me]
+        to_ctx(dt_own.at[d], dt_all.at[me], dt_send.at[k], dt_recv.at[me], d).start()
+    dt_all[me] = dt_own[me]
 
     starts = []
     total = jnp.int32(0)
@@ -418,14 +427,11 @@
     tap_count = taps_ref.shape[0]
     since = own_pos - own_first
 
-    def conv(extended, taps, wide):
+    def conv(extended, taps):
         acc = None
         for m in range(tap_count):
             part = extended[8 - m: 8 - m + rows] * taps[tap_count - 1 - m: tap_count - m]
-            seen = since >= m
-            if wide > 1:
-                seen = jnp.concatenate([seen.astype(jnp.int32)] * wide, axis=1) > 0
-            part = jnp.where(seen, part, 0.0)
+            part = jnp.where(since >= m, part, 0.0)
             acc = part if acc is None else acc + part
         return silu(acc).astype(jnp.bfloat16)
 
@@ -439,7 +445,13 @@
                 (i * groups + group) * state_size + piece * LANES, LANES), LANES)
             extended = jnp.concatenate(
                 [bc_rim[:, cols].astype(jnp.float32)[RIM - 8:], bc_ref[:, cols].astype(jnp.float32)], axis=0)
-            bc_all[me, i, :, piece * LANES:(piece + 1) * LANES] = conv(extended, bc_taps_ref[:, cols], 1)
+            lanes = slice(piece * LANES, (piece + 1) * LANES)
+            taps = jnp.zeros((tap_count, LANES), jnp.float32)
+            for g in range(groups):
+                part = jnp.concatenate(
+                    [bc_taps_ref[m, i, g:g + 1, lanes] for m in range(tap_count)], axis=0)
+                taps = jnp.where(group == g, part, taps)
+            bc_all[me, i, :, piece * LANES:(piece + 1) * LANES] = conv(extended, taps)
 
     column = [lax.rem(me + 2 * k, n) for k in range(1, n // 2)]
 
@@ -471,9 +483,8 @@
         @pl.when(odd & (me >= r))
         def _():
             relay_odd[r // 2 - 1].start()
-        if r == 2:
-            for copy in bc_own:
-                copy.start()
+    for copy in bc_own:
+        copy.start()
     for r in range(1, window, 2):
         @pl.when(me >= r)
         def _():
@@ -485,7 +496,8 @@
 
     keys = jnp.concatenate([kv[r, 0] for r in range(window)], axis=0)
     values = jnp.concatenate([kv[r, 1] for r in range(window)], axis=0)
-    scale = 1.0 / math.sqrt(k_ref.shape[1])
+    values = jnp.concatenate([values, jnp.ones_like(values)], axis=1)
+    scale = math.log2(math.e) / math.sqrt(k_ref.shape[1])
 
     def bias_of(pos):
         first = first_of(pos)
@@ -496,11 +508,10 @@
         return jnp.concatenate(parts, axis=1)
 
     def attention(block, bias):
-        scores = dot_nt(block, keys) * scale + bias
-        exponent = jnp.exp(scores - jnp.max(scores, axis=1, keepdims=True))
-        totals = jnp.sum(exponent, axis=1, keepdims=True)
+        scores = dot_nt(block, keys) + bias
+        exponent = jnp.exp2((scores - jnp.max(scores, axis=1, keepdims=True)) * scale)
         summed = dot_nn(exponent.astype(jnp.bfloat16), values)
-        return (summed / totals).astype(jnp.bfloat16).astype(jnp.float32)
+        return (summed[:, :LANES] / summed[:, LANES:]).astype(jnp.bfloat16).astype(jnp.float32)
 
     rim_block = jnp.concatenate(
         [q_rim[:, h * LANES:(h + 1) * LANES] for h in range(n)], axis=0)
@@ -516,7 +527,7 @@
         cols = pl.ds(pl.multiple_of(h * LANES, LANES), LANES)
         attended = attention(q_ref[:, cols], bias)
         rim = gated_ref[0, pl.ds(pl.multiple_of(h * RIM + RIM - 8, 8), 8), :]
-        x = conv(jnp.concatenate([rim, attended], axis=0), taps_ref[:, cols], 1)
+        x = conv(jnp.concatenate([rim, attended], axis=0), taps_ref[:, cols])
         if k < n - 1:
             x_out[h] = x
             to_ctx(x_out.at[h], x_all.at[me], x_send.at[k], x_recv.at[me], h).start()
@@ -538,22 +549,18 @@
     skip = jnp.where(left[:1], skip_ref[2 * me], skip_ref[2 * me + 1])
     for k in range(1, n):
         s = lax.rem(me + k, n)
-        to_ctx(dt_ref.at[s], dt_all.at[s], dt_send.at[k], dt_recv.at[s], s).wait_recv()
+        to_ctx(dt_own.at[s], dt_all.at[s], dt_send.at[k], dt_recv.at[s], s).wait_recv()
     dt_rows = [jnp.concatenate([dt_all[i, a:a + 1] for i in range(n)], axis=0) for a in range(2)]
     cum_rows = [jnp.dot(-rate[a] * dt_rows[a], upper, precision=lax.Precision.HIGHEST,
                         preferred_element_type=jnp.float32) for a in range(2)]
-    state = jnp.zeros((state_size, LANES), jnp.float32)
+    keeps = []
     for i in range(n):
         @pl.when(me != i)
         def _():
-            to_ctx(x_all.at[i], x_all.at[i], x_send.at[0], x_recv.at[i], pair).wait_recv()
             other = 1 - core
             to_core(bc_all.at[i, other], bc_all.at[i, other], bc_core_send.at[0],
                     bc_core_recv.at[i]).wait_recv()
 
-        x = x_all[i]
-        b, c = bc_all[i, 0], bc_all[i, 1]
-        xw = x.astype(jnp.float32)
         start = i * rows
         pos = start + row_iota
         first = first_of(pos)
@@ -564,42 +571,47 @@
         side = (rows // 2, LANES)
         cum_col = jnp.concatenate([jnp.broadcast_to(r, side) for r in cum], axis=0).T
         dt_col = jnp.concatenate([jnp.broadcast_to(r, side) for r in dts], axis=0).T
-        gram = jnp.where(visible, dot_nt(c, b), 0.0)
-        mix = []
+        gram = jnp.where(visible, dot_nt(bc_all[i, 1], bc_all[i, 0]), 0.0)
         for a in range(2):
             col = cum_col[:, a * (LANES // 2):a * (LANES // 2) + 1]
             gap = jnp.where(visible, col - cum[a], 0.0)
-            mix.append((gram * jnp.exp(gap) * dts[a]).astype(jnp.bfloat16))
+            mix_ref[i, :, a * LANES:(a + 1) * LANES] = (
+                gram * jnp.exp(gap) * dts[a]).astype(jnp.bfloat16)
+        last_start = first[rows - 1:rows]
+        cum_last = cum_col[rows - 1:rows]
+        carry_ref[i] = jnp.where(first < start, jnp.exp(cum_col), 0.0)
+        weight_ref[i] = jnp.where(pos >= last_start, jnp.exp(cum_last - cum_col) * dt_col, 0.0)
+        keeps.append(jnp.where(last_start < start, jnp.exp(cum_last), 0.0))
+
+    state = jnp.zeros((state_size, LANES), jnp.float32)
+    for i in range(n):
+        @pl.when(me != i)
+        def _():
+            to_ctx(x_all.at[i], x_all.at[i], x_send.at[0], x_recv.at[i], pair).wait_recv()
+
+        state_ref[i] = state.astype(jnp.bfloat16)
+        if i < n - 1:
+            weighted = (x_all[i].astype(jnp.float32) * weight_ref[i]).astype(jnp.bfloat16)
+            state = keeps[i] * state + dot_tn(bc_all[i, 0], weighted)
+
+    for k in range(n):
+        i = lax.rem(me + 1 + k, n)
+        xw = x_all[i].astype(jnp.float32)
         both = jnp.concatenate([jnp.where(left, xw, 0.0), jnp.where(left, 0.0, xw)], axis=0)
-        y = dot_nn(jnp.concatenate(mix, axis=1), both.astype(jnp.bfloat16)) + skip * xw
-        if i > 0:
-            carried = dot_nn(c, state.astype(jnp.bfloat16))
-            y = y + jnp.where(first < start, jnp.exp(cum_col), 0.0) * carried
-        if i < n - 1:
-            last_start = first[rows - 1:rows]
-            cum_last = cum_col[rows - 1:rows]
-            weight = jnp.where(pos >= last_start, jnp.exp(cum_last - cum_col) * dt_col, 0.0)
-            grown = dot_tn(b, (xw * weight).astype(jnp.bfloat16))
-            keep = jnp.where(last_start < start, jnp.exp(cum_last), 0.0)
-            state = keep * state + grown
-        y = y.astype(jnp.bfloat16)
-
-        @pl.when(me != i)
-        def _():
+        y = dot_nn(mix_ref[i], both.astype(jnp.bfloat16)) + skip * xw
+        y = (y + carry_ref[i] * dot_nn(bc_all[i, 1], state_ref[i])).astype(jnp.bfloat16)
+        if k < n - 1:
             y_out[i] = y
             to_ctx(y_out.at[i], y_all.at[me], y_send.at[i], y_recv.at[me], i).start()
-
-        @pl.when(me == i)
-        def _():
+        else:
             y_all[me] = y
 
     squares = jnp.zeros((rows, LANES), jnp.float32)
-    for h in range(n):
-        @pl.when(me != h)
-        def _():
-            to_ctx(y_out.at[h], y_all.at[h], y_send.at[h], y_recv.at[h], pair).wait_recv()
-
-        z = gate_ref[:, h * LANES:(h + 1) * LANES].astype(jnp.float32)
+    for k in range(n):
+        h = lax.rem(me + n - 1 - k, n)
+        if k < n - 1:
+            to_ctx(y_out.at[h], y_all.at[h], y_send.at[h], y_recv.at[h], h).wait_recv()
+        z = gate_ref[:, pl.ds(pl.multiple_of(h * LANES, LANES), LANES)].astype(jnp.float32)
         gated = y_all[h].astype(jnp.float32) * silu(z)
         gated_ref[h] = gated
         squares = squares + gated * gated
@@ -634,7 +646,7 @@
     for k in range(n - 1):
         h = lax.rem(me + 1 + k, n)
         to_ctx(x_out.at[h], x_all.at[me], x_send.at[k], x_recv.at[me], h).wait_send()
-        to_ctx(dt_ref.at[h], dt_all.at[me], dt_send.at[k + 1], dt_recv.at[me], h).wait_send()
+        to_ctx(dt_own.at[h], dt_all.at[me], dt_send.at[k + 1], dt_recv.at[me], h).wait_send()
     for i in range(n):
         @pl.when(me != i)
         def _():
@@ -658,7 +670,6 @@
     longest = n * rows // 2 + 64
     window = 1 + -(-(longest - 1) // rows)
     bc = bc_input.reshape(rows, -1)
-    dt = jnp.pad(step_size.T.reshape(n, 2, rows), ((0, 0), (0, 6), (0, 0)))
     bf16, f32 = jnp.bfloat16, jnp.float32
     vmem = pl.BlockSpec(memory_space=pltpu.VMEM)
     smem = pl.BlockSpec(memory_space=pltpu.SMEM)
@@ -677,6 +688,11 @@
             pltpu.VMEM((n, rows, LANES), bf16),
             pltpu.VMEM((n, rows, LANES), bf16),
             pltpu.VMEM((n, 8, LANES), f32),
+            pltpu.VMEM((n, 8, LANES), f32),
+            pltpu.VMEM((n, rows, 2 * LANES), bf16),
+            pltpu.VMEM((n, rows, LANES), f32),
+            pltpu.VMEM((n, rows, LANES), f32),
+            pltpu.VMEM((n, state_size, LANES), bf16),
             pltpu.VMEM((n, rows, LANES), bf16),
             pltpu.VMEM((n, rows, LANES), bf16),
             pltpu.VMEM((n, rows, LANES), f32),
@@ -701,8 +717,8 @@
         compiler_params=pltpu.CompilerParams(
             collective_id=0, has_side_effects=True, vmem_limit_bytes=32 * 1024 * 1024),
     )(
-        doc_lengths, decay_rate, skip_gain, queries, key_rows, value_rows, gate_input, bc, dt,
-        conv_x, conv_bc.reshape(conv_bc.shape[0], -1), norm_gain.reshape(1, -1),
+        doc_lengths, decay_rate, skip_gain, queries, key_rows, value_rows, gate_input, bc, step_size.T,
+        conv_x, conv_bc, norm_gain.reshape(1, -1),
     )
 
 

time: 41.8 us -> 47.9 us (1.15)
  local copies, waits for them, and re-layouts: 4.1 us -> 8.18 us
  Pallas kernels: 37.2 us -> 39.2 us
    unnamed x19 -> x23, local copies, waits for them, and re-layouts: 1.46 us -> 7 us
    pallas_call x1, Pallas kernels: 37.2 us -> 39.2 us  [fused_on_device(): pl.pallas_call(functools.partial(fused_kernel, n, window), out_shape=jax....]
    reshape x1 -> x0, local copies, waits for them, and re-layouts: 0.75 us -> none  [fused_on_device(): conv_bc.reshape(conv_bc.shape[0], -1)]
    pad x1 -> x0, local copies, waits for them, and re-layouts: 0.72 us -> none  [fused_on_device(): dt = jnp.pad(step_size.T.reshape(n, 2, rows), ((0, 0), (0, 6), (0, 0)))]
where the time goes in v2:
time: 47.9 us; the launch traced here: 47.4 us
  Pallas kernels  39.2 us (82%)
  local copies, waits for them, and re-layouts  8.18 us (17%)
    pallas_call x1, Pallas kernels, fused_on_device(): pl.pallas_call(functools.partial(fused_kernel, n, window), out_shape=jax....  39.2 us
    unnamed x23, local copies, waits for them, and re-layouts  7 us
    reshape x1, local copies, waits for them, and re-layouts, fused_on_device(): bc = bc_input.reshape(rows, -1)  1.17 us

profile of v2, /device:TPU:0, one launch (start us, length us, event | category | flops | bytes accessed | tf_op | source)
XLA Modules:
  0.0 47.4 jit_solution(16501738234065408860)
XLA Ops:
  0.0 0.0 copy-start
  0.0 0.0 copy-start.1
  0.0 1.2 %reshape.6.bc_ref = bf16[128,1024]{1,0:T(8,128)(2,1)S(1)} reshape(bf16[128,2,2,256]{3,2,1,0:T(2,128)(2,1)} %param.17) | data formatting | bytes 524288 | tf_op jit(solution)/shard_map/reshape | solution.py:672
  1.2 0.0 copy-done
  1.2 0.0 copy-done.1
  1.2 0.0 copy-start.2
  1.2 0.7 %copy-done.2 = bf16[128,128]{1,0:T(8,128)(2,1)S(1)} copy-done((bf16[128,128]{1,0:T(8,128)(2,1)S(1)}, bf16[128,128]{1,0:T(8,128)(2,1)}, u32[]{:S(2)}) %copy-start.2) | copy-done | bytes 32792
  2.0 0.0 copy-start.3
  2.0 0.8 %copy-done.3 = bf16[128,128]{1,0:T(8,128)(2,1)S(1)} copy-done((bf16[128,128]{1,0:T(8,128)(2,1)S(1)}, bf16[128,128]{1,0:T(8,128)(2,1)}, u32[]{:S(2)}) %copy-start.3) | copy-done | bytes 32792
  2.7 0.0 copy-start.4
  2.7 0.7 %copy-done.4 = f32[4,1024]{1,0:T(4,128)S(1)} copy-done((f32[4,1024]{1,0:T(4,128)S(1)}, f32[4,1024]{1,0:T(4,128)}, u32[]{:S(2)}) %copy-start.4) | copy-done | bytes 16408
  3.4 0.0 copy-start.5
  3.4 0.7 %copy-done.5 = f32[4,2,2,256]{3,2,1,0:T(2,128)S(1)} copy-done((f32[4,2,2,256]{3,2,1,0:T(2,128)S(1)}, f32[4,2,2,256]{3,2,1,0:T(2,128)}, u32[]{:S(2)}) %copy-start.5) | copy-done | bytes 16408
  4.2 0.0 copy-start.6
  4.2 0.7 %copy-done.6 = f32[128,16]{0,1:T(8,128)S(1)} copy-done((f32[128,16]{0,1:T(8,128)S(1)}, f32[128,16]{0,1:T(8,128)}, u32[]{:S(2)}) %copy-start.6) | copy-done | bytes 8216
  4.9 0.0 copy-start.7
  4.9 0.7 %copy-done.7 = f32[1024]{0:T(1024)S(1)} copy-done((f32[1024]{0:T(1024)S(1)}, f32[1024]{0:T(1024)}, u32[]{:S(2)}) %copy-start.7) | copy-done | bytes 4120
  5.5 0.0 copy-start.8
  5.5 0.7 %copy-done.8 = s32[4]{0:T(128)S(1)} copy-done((s32[4]{0:T(128)S(1)}, s32[4]{0:T(128)}, u32[]{:S(2)}) %copy-start.8) | copy-done | bytes 40
  6.2 0.0 copy-start.9
  6.2 0.7 %copy-done.9 = f32[16]{0:T(128)S(1)} copy-done((f32[16]{0:T(128)S(1)}, f32[16]{0:T(128)}, u32[]{:S(2)}) %copy-start.9) | copy-done | bytes 88
  6.9 0.7 %copy-done.10 = f32[16]{0:T(128)S(1)} copy-done((f32[16]{0:T(128)S(1)}, f32[16]{0:T(128)}, u32[]{:S(2)}) %copy-start.10) | copy-done | bytes 88
  7.5 39.2 %shard_map.118 = bf16[128,1024]{1,0:T(8,128)(2,1)S(1)} custom-call(s32[4]{0:T(128)S(1)} %copy-done.8, f32[16]{0:T(128)S(1)} %copy-done.9, f32[16]{0:T(128)S(1)} %copy-done.10, bf16[128,1024]{1,0:T(8,128)(2,1)S(1)} %copy-done, bf16[128,128]{1,0:T(8,128)(2,1)S(1)} %copy-done.2, bf16[128,128]{1,0:T(8,128)(2,1)S(1)} %copy-done.3, ...), custom_call_target="tpu_custom_call" | custom-call | tf_op jit(solution)/shard_map/pallas_call | solution.py:678
  46.7 0.7 %copy.14 = bf16[128,1024]{1,0:T(8,128)(2,1)} copy(bf16[128,1024]{1,0:T(8,128)(2,1)S(1)} %shard_map.118) | data formatting | bytes 524288
  (1 shorter events, 0.0 us)
Async XLA Ops:
  0.0 1.2 %copy-start = (bf16[128,1024]{1,0:T(8,128)(2,1)S(1)}, bf16[128,1024]{1,0:T(8,128)(2,1)}, u32[]{:S(2)}) copy-start(bf16[128,1024]{1,0:T(8,128)(2,1)} %q_ref.1) | copy-start | bytes 786436
  0.0 1.2 %copy-start.1 = (bf16[128,1024]{1,0:T(8,128)(2,1)S(1)}, bf16[128,1024]{1,0:T(8,128)(2,1)}, u32[]{:S(2)}) copy-start(bf16[128,1024]{1,0:T(8,128)(2,1)} %gate_ref.1) | copy-start | bytes 786436
  1.2 0.8 %copy-start.2 = (bf16[128,128]{1,0:T(8,128)(2,1)S(1)}, bf16[128,128]{1,0:T(8,128)(2,1)}, u32[]{:S(2)}) copy-start(bf16[128,128]{1,0:T(8,128)(2,1)} %k_ref.1) | copy-start | bytes 98308
  2.0 0.8 %copy-start.3 = (bf16[128,128]{1,0:T(8,128)(2,1)S(1)}, bf16[128,128]{1,0:T(8,128)(2,1)}, u32[]{:S(2)}) copy-start(bf16[128,128]{1,0:T(8,128)(2,1)} %v_ref.1) | copy-start | bytes 98308
  2.7 0.7 %copy-start.4 = (f32[4,1024]{1,0:T(4,128)S(1)}, f32[4,1024]{1,0:T(4,128)}, u32[]{:S(2)}) copy-start(f32[4,1024]{1,0:T(4,128)} %taps_ref.1) | copy-start | bytes 49156
  3.4 0.7 %copy-start.5 = (f32[4,2,2,256]{3,2,1,0:T(2,128)S(1)}, f32[4,2,2,256]{3,2,1,0:T(2,128)}, u32[]{:S(2)}) copy-start(f32[4,2,2,256]{3,2,1,0:T(2,128)} %bc_taps_ref.1) | copy-start | bytes 49156
  4.2 0.7 %copy-start.6 = (f32[128,16]{0,1:T(8,128)S(1)}, f32[128,16]{0,1:T(8,128)}, u32[]{:S(2)}) copy-start(f32[128,16]{0,1:T(8,128)} %param.18) | copy-start | bytes 24580
  4.9 0.7 %copy-start.7 = (f32[1024]{0:T(1024)S(1)}, f32[1024]{0:T(1024)}, u32[]{:S(2)}) copy-start(f32[1024]{0:T(1024)} %param.23) | copy-start | bytes 12292
  5.5 0.7 %copy-start.8 = (s32[4]{0:T(128)S(1)}, s32[4]{0:T(128)}, u32[]{:S(2)}) copy-start(s32[4]{0:T(128)} %doc_ref.1) | copy-start | bytes 52
  6.2 0.7 %copy-start.9 = (f32[16]{0:T(128)S(1)}, f32[16]{0:T(128)}, u32[]{:S(2)}) copy-start(f32[16]{0:T(128)} %rate_ref.1) | copy-start | bytes 196
  6.9 0.7 %copy-start.10 = (f32[16]{0:T(128)S(1)}, f32[16]{0:T(128)}, u32[]{:S(2)}) copy-start(f32[16]{0:T(128)} %skip_ref.1) | copy-start | bytes 196

commit v3 on v2

--- a/solution.py
+++ b/solution.py
@@ -278,16 +278,24 @@
     doc_ref,
     rate_ref,
     skip_ref,
+    q_in,
+    k_in,
+    v_in,
+    gate_in,
+    bc_in,
+    step_in,
+    taps_in,
+    bc_taps_in,
+    gain_in,
+    out_ref,
     q_ref,
-    k_ref,
-    v_ref,
     gate_ref,
     bc_ref,
     step_ref,
     taps_ref,
     bc_taps_ref,
     gain_ref,
-    out_ref,
+    load_sem,
     kv,
     q_rim,
     bc_rim,
@@ -321,6 +329,15 @@
     y_recv,
     sq_sem,
 ):
+    loads = [
+        pltpu.make_async_copy(src, dst, load_sem.at[i])
+        for i, (src, dst) in enumerate((
+            (k_in, kv.at[0, 0]), (v_in, kv.at[0, 1]), (bc_in, bc_ref), (q_in, q_ref),
+            (step_in, step_ref), (bc_taps_in, bc_taps_ref), (taps_in, taps_ref),
+            (gate_in, gate_ref), (gain_in, gain_ref)))
+    ]
+    for load in loads:
+        load.start()
     rows = q_ref.shape[0]
     me = lax.axis_index("ctx")
     tp = lax.axis_index("tp")
@@ -348,8 +365,6 @@
         pl.semaphore_signal(
             barrier, inc=1, device_id=(lax.rem(me + k, n), tp), device_id_type=MESH)
     pl.semaphore_signal(barrier, inc=1, device_id=(me, tp_other), device_id_type=MESH)
-    kv[0, 0] = k_ref[...]
-    kv[0, 1] = v_ref[...]
     for r in range(1, window):
         @pl.when(me < r)
         def _():
@@ -360,6 +375,8 @@
         q_rim[...] = jnp.zeros(q_rim.shape, q_rim.dtype)
         bc_rim[...] = jnp.zeros(bc_rim.shape, bc_rim.dtype)
 
+    for load in loads:
+        load.wait()
     steps = step_ref[...]
     for d in range(n):
         dt_own[d, 0:2] = steps[2 * d:2 * d + 2]
@@ -475,6 +492,9 @@
         def _():
             to_ctx(kv.at[0], kv.at[r], kv_send.at[0], kv_recv.at[r], pair).wait_recv()
 
+        if r == 2:
+            for copy in bc_own:
+                copy.start()
         if r < window:
             @pl.when(even & (me >= r))
             def _():
@@ -483,8 +503,6 @@
         @pl.when(odd & (me >= r))
         def _():
             relay_odd[r // 2 - 1].start()
-    for copy in bc_own:
-        copy.start()
     for r in range(1, window, 2):
         @pl.when(me >= r)
         def _():
@@ -497,7 +515,7 @@
     keys = jnp.concatenate([kv[r, 0] for r in range(window)], axis=0)
     values = jnp.concatenate([kv[r, 1] for r in range(window)], axis=0)
     values = jnp.concatenate([values, jnp.ones_like(values)], axis=1)
-    scale = math.log2(math.e) / math.sqrt(k_ref.shape[1])
+    scale = math.log2(math.e) / math.sqrt(k_in.shape[1])
 
     def bias_of(pos):
         first = first_of(pos)
@@ -522,6 +540,7 @@
     def recv_bc(s):
         to_ctx(bc_all.at[s, core], bc_all.at[s, core], bc_send.at[0], bc_recv.at[s], pair).wait_recv()
 
+    crossed = [pair] + [lax.rem(pair + 2 * k, n) for k in range(1, n // 2)]
     for k in range(n):
         h = lax.rem(me + 1 + k, n)
         cols = pl.ds(pl.multiple_of(h * LANES, LANES), LANES)
@@ -533,15 +552,15 @@
             to_ctx(x_out.at[h], x_all.at[me], x_send.at[k], x_recv.at[me], h).start()
         else:
             x_all[me] = x
-        if k >= n // 2 and k - n // 2 < len(column):
-            s = column[k - n // 2]
+        if 1 <= k <= len(column):
+            s = column[k - 1]
             recv_bc(s)
-            relay_bc(s, n // 2 + k - n // 2).start()
-            share_bc(s, k - n // 2).start()
-    crossed = [pair] + [lax.rem(pair + 2 * k, n) for k in range(1, n // 2)]
-    for k, s in enumerate(crossed):
-        recv_bc(s)
-        share_bc(s, n // 2 - 1 + k).start()
+            relay_bc(s, n // 2 + k - 1).start()
+            share_bc(s, k - 1).start()
+        if n // 2 <= k:
+            s = crossed[k - n // 2]
+            recv_bc(s)
+            share_bc(s, k - 1).start()
 
     upper = (row_iota <= lane_iota).astype(jnp.float32)
     left = lane_iota < LANES // 2
@@ -554,13 +573,12 @@
     cum_rows = [jnp.dot(-rate[a] * dt_rows[a], upper, precision=lax.Precision.HIGHEST,
                         preferred_element_type=jnp.float32) for a in range(2)]
     keeps = []
+    other = 1 - core
+    for k in range(1, n):
+        s = lax.rem(me + k, n)
+        to_core(bc_all.at[s, other], bc_all.at[s, other], bc_core_send.at[0],
+                bc_core_recv.at[s]).wait_recv()
     for i in range(n):
-        @pl.when(me != i)
-        def _():
-            other = 1 - core
-            to_core(bc_all.at[i, other], bc_all.at[i, other], bc_core_send.at[0],
-                    bc_core_recv.at[i]).wait_recv()
-
         start = i * rows
         pos = start + row_iota
         first = first_of(pos)
@@ -584,11 +602,10 @@
         keeps.append(jnp.where(last_start < start, jnp.exp(cum_last), 0.0))
 
     state = jnp.zeros((state_size, LANES), jnp.float32)
+    for k in range(1, n):
+        s = lax.rem(me + n - k, n)
+        to_ctx(x_all.at[s], x_all.at[s], x_send.at[0], x_recv.at[s], pair).wait_recv()
     for i in range(n):
-        @pl.when(me != i)
-        def _():
-            to_ctx(x_all.at[i], x_all.at[i], x_send.at[0], x_recv.at[i], pair).wait_recv()
-
         state_ref[i] = state.astype(jnp.bfloat16)
         if i < n - 1:
             weighted = (x_all[i].astype(jnp.float32) * weight_ref[i]).astype(jnp.bfloat16)
@@ -678,9 +695,17 @@
     return pl.pallas_call(
         functools.partial(fused_kernel, n, window),
         out_shape=jax.ShapeDtypeStruct(queries.shape, bf16),
-        in_specs=[smem] * 3 + [vmem] * 9,
+        in_specs=[smem] * 3 + [pl.BlockSpec(memory_space=pl.ANY)] * 9,
         out_specs=vmem,
         scratch_shapes=[
+            pltpu.VMEM(queries.shape, bf16),
+            pltpu.VMEM(gate_input.shape, bf16),
+            pltpu.VMEM(bc.shape, bf16),
+            pltpu.VMEM(step_size.shape[::-1], f32),
+            pltpu.VMEM(conv_x.shape, f32),
+            pltpu.VMEM(conv_bc.shape, f32),
+            pltpu.VMEM((1, norm_gain.shape[0]), f32),
+            dma((9,)),
             pltpu.VMEM((window + 1, 2, rows, LANES), bf16),
             pltpu.VMEM((RIM, queries.shape[1]), bf16),
             pltpu.VMEM((RIM, bc.shape[1]), bf16),
@@ -715,7 +740,7 @@
             dma((2,)),
         ],
         compiler_params=pltpu.CompilerParams(
-            collective_id=0, has_side_effects=True, vmem_limit_bytes=32 * 1024 * 1024),
+            collective_id=0, has_side_effects=True, vmem_limit_bytes=58 * 1024 * 1024),
     )(
         doc_lengths, decay_rate, skip_gain, queries, key_rows, value_rows, gate_input, bc, step_size.T,
         conv_x, conv_bc, norm_gain.reshape(1, -1),

time: 47.9 us -> 43.3 us (0.904)
  local copies, waits for them, and re-layouts: 8.18 us -> 3.49 us
    unnamed x23 -> x1, local copies, waits for them, and re-layouts: 7 us -> 1.67 us
    reshape x1, local copies, waits for them, and re-layouts: 1.17 us -> 1.82 us  [fused_on_device(): bc = bc_input.reshape(rows, -1)]
where the time goes in v3:
time: 43.3 us; the launch traced here: 43.1 us
  Pallas kernels  39.6 us (91%)
  local copies, waits for them, and re-layouts  3.49 us (8%)
    pallas_call x1, Pallas kernels, fused_on_device(): pl.pallas_call(functools.partial(fused_kernel, n, window), out_shape=jax....  39.6 us
    reshape x1, local copies, waits for them, and re-layouts, fused_on_device(): bc = bc_input.reshape(rows, -1)  1.82 us
    unnamed x1, local copies, waits for them, and re-layouts  1.67 us

profile of v3, /device:TPU:0, one launch (start us, length us, event | category | flops | bytes accessed | tf_op | source)
XLA Modules:
  0.0 43.1 jit_solution(1385059824116028909)
XLA Ops:
  0.0 1.8 %reshape.6.bc_in = bf16[128,1024]{1,0:T(8,128)(2,1)} reshape(bf16[128,2,2,256]{3,2,1,0:T(2,128)(2,1)} %param.17) | data formatting | bytes 524288 | tf_op jit(solution)/shard_map/reshape | solution.py:689
  1.8 39.6 %shard_map.118 = bf16[128,1024]{1,0:T(8,128)(2,1)} custom-call(s32[4]{0:T(128)} %doc_ref.1, f32[16]{0:T(128)} %rate_ref.1, f32[16]{0:T(128)} %skip_ref.1, bf16[128,1024]{1,0:T(8,128)(2,1)} %q_in.1, bf16[128,128]{1,0:T(8,128)(2,1)} %k_in.1, bf16[128,128]{1,0:T(8,128)(2,1)} %v_in.1, bf16[128,1024]{1,0:T(8,128)(2,1)} %gate_in.1, ...), custom_call_target="tpu_custom_call" | custom-call | tf_op jit(solution)/shard_map/pallas_call | solution.py:695
  41.4 1.7 %copy.14 = bf16[128,1024]{1,0:T(8,128)(2,1)} copy(bf16[128,1024]{1,0:T(8,128)(2,1)} %shard_map.118) | data formatting | bytes 524288

commit v4 on v3

--- a/solution.py
+++ b/solution.py
@@ -318,6 +318,7 @@
     rim_send,
     rim_recv,
     bc_send,
+    bc_pass,
     bc_recv,
     bc_core_send,
     bc_core_recv,
@@ -386,9 +387,9 @@
     half = window // 2
     direct = []
     for k in range(1, half + 1):
-        copy = to_ctx(kv.at[0], kv.at[2 * k], kv_send.at[k], kv_recv.at[2 * k],
-                      jnp.minimum(me + 2 * k, n - 1))
-        wanted = me + 2 * k < n
+        copy = to_ctx(kv.at[2 * k - 2], kv.at[2 * k], kv_send.at[k], kv_recv.at[2 * k],
+                      jnp.minimum(me + 2, n - 1))
+        wanted = (me + 2 < n) & (me >= 2 * k - 2)
         if 2 * k >= window:
             wanted = wanted & (parity == 1)
         direct.append((wanted, copy))
@@ -410,10 +411,9 @@
     def _():
         relay_even[0].start()
 
-    for wanted, copy in direct:
-        @pl.when(wanted)
-        def _():
-            copy.start()
+    @pl.when(direct[0][0])
+    def _():
+        direct[0][1].start()
 
     @pl.when(me + 1 < n)
     def _():
@@ -470,18 +470,21 @@
                 taps = jnp.where(group == g, part, taps)
             bc_all[me, i, :, piece * LANES:(piece + 1) * LANES] = conv(extended, taps)
 
-    column = [lax.rem(me + 2 * k, n) for k in range(1, n // 2)]
-
-    def relay_bc(s, slot):
-        return to_ctx(bc_all.at[s, core], bc_all.at[s, core], bc_send.at[slot], bc_recv.at[s], pair)
-
-    def share_bc(s, slot):
-        return to_core(bc_all.at[s, core], bc_all.at[s, core], bc_core_send.at[slot], bc_core_recv.at[s])
-
-    bc_own = [to_ctx(bc_all.at[me, core], bc_all.at[me, core], bc_send.at[0], bc_recv.at[me], pair)]
-    for k, d in enumerate(column):
-        bc_own.append(to_ctx(bc_all.at[me, core], bc_all.at[me, core],
-                             bc_send.at[1 + k], bc_recv.at[me], d))
+    def bc_copy(s, sem, where):
+        return to_ctx(bc_all.at[s, core], bc_all.at[s, core], sem, bc_recv.at[s], where)
+
+    def share_bc(s):
+        return to_core(bc_all.at[s, core], bc_all.at[s, core], bc_core_send.at[s], bc_core_recv.at[s])
+
+    has_up, has_down = me + 2 < n, me >= 2
+    above, below = jnp.minimum(me + 2, n - 1), jnp.maximum(me - 2, 0)
+    bc_pair = bc_copy(me, bc_send.at[me], pair)
+    bc_up = bc_copy(me, bc_pass.at[me], above)
+    bc_down = bc_copy(me, bc_pass.at[n], below)
+    column = []
+    for k in range(1, n // 2):
+        column.append((me >= 2 * k, jnp.maximum(me - 2 * k, 0), has_up, above))
+        column.append((me + 2 * k < n, jnp.minimum(me + 2 * k, n - 1), has_down, below))
 
     for r in range(2, window + 1, 2):
         cond = me >= r
@@ -492,9 +495,20 @@
         def _():
             to_ctx(kv.at[0], kv.at[r], kv_send.at[0], kv_recv.at[r], pair).wait_recv()
 
+        if r // 2 < len(direct):
+            @pl.when(direct[r // 2][0])
+            def _():
+                direct[r // 2][1].start()
         if r == 2:
-            for copy in bc_own:
-                copy.start()
+            bc_pair.start()
+
+            @pl.when(has_up)
+            def _():
+                bc_up.start()
+
+            @pl.when(has_down)
+            def _():
+                bc_down.start()
         if r < window:
             @pl.when(even & (me >= r))
             def _():
@@ -552,15 +566,22 @@
             to_ctx(x_out.at[h], x_all.at[me], x_send.at[k], x_recv.at[me], h).start()
         else:
             x_all[me] = x
-        if 1 <= k <= len(column):
-            s = column[k - 1]
-            recv_bc(s)
-            relay_bc(s, n // 2 + k - 1).start()
-            share_bc(s, k - 1).start()
+        if 1 <= k < n // 2:
+            for here, s, onward, where in column[2 * k - 2:2 * k]:
+                @pl.when(here)
+                def _():
+                    recv_bc(s)
+
+                    @pl.when(onward)
+                    def _():
+                        bc_copy(s, bc_pass.at[s], where).start()
+
+                    bc_copy(s, bc_send.at[s], pair).start()
+                    share_bc(s).start()
         if n // 2 <= k:
             s = crossed[k - n // 2]
             recv_bc(s)
-            share_bc(s, k - 1).start()
+            share_bc(s).start()
 
     upper = (row_iota <= lane_iota).astype(jnp.float32)
     left = lane_iota < LANES // 2
@@ -653,13 +674,26 @@
     def _():
         rim_q.wait_send()
         rim_b.wait_send()
-    for copy in bc_own:
-        copy.wait_send()
-    for k, s in enumerate(column):
-        relay_bc(s, n // 2 + k).wait_send()
-        share_bc(s, k).wait_send()
-    for k, s in enumerate(crossed):
-        share_bc(s, n // 2 - 1 + k).wait_send()
+    bc_pair.wait_send()
+
+    @pl.when(has_up)
+    def _():
+        bc_up.wait_send()
+
+    @pl.when(has_down)
+    def _():
+        bc_down.wait_send()
+    for here, s, onward, where in column:
+        @pl.when(here)
+        def _():
+            bc_copy(s, bc_send.at[s], pair).wait_send()
+            share_bc(s).wait_send()
+
+            @pl.when(onward)
+            def _():
+                bc_copy(s, bc_pass.at[s], where).wait_send()
+    for s in crossed:
+        share_bc(s).wait_send()
     for k in range(n - 1):
         h = lax.rem(me + 1 + k, n)
         to_ctx(x_out.at[h], x_all.at[me], x_send.at[k], x_recv.at[me], h).wait_send()
@@ -688,6 +722,7 @@
     window = 1 + -(-(longest - 1) // rows)
     bc = bc_input.reshape(rows, -1)
     bf16, f32 = jnp.bfloat16, jnp.float32
+    hbm = pl.BlockSpec(memory_space=pl.ANY)
     vmem = pl.BlockSpec(memory_space=pltpu.VMEM)
     smem = pl.BlockSpec(memory_space=pltpu.SMEM)
     dma = pltpu.SemaphoreType.DMA
@@ -695,7 +730,7 @@
     return pl.pallas_call(
         functools.partial(fused_kernel, n, window),
         out_shape=jax.ShapeDtypeStruct(queries.shape, bf16),
-        in_specs=[smem] * 3 + [pl.BlockSpec(memory_space=pl.ANY)] * 9,
+        in_specs=[smem] * 3 + [hbm] * 9,
         out_specs=vmem,
         scratch_shapes=[
             pltpu.VMEM(queries.shape, bf16),
@@ -728,6 +763,7 @@
             dma((2,)),
             dma((2,)),
             dma((n,)),
+            dma((n + 1,)),
             dma((n,)),
             dma((n,)),
             dma((n,)),

time: 43.3 us -> 44.3 us (1.023)
  Pallas kernels: 39.6 us -> 40.6 us
    pallas_call x1, Pallas kernels: 39.6 us -> 40.6 us  [fused_on_device(): pl.pallas_call(functools.partial(fused_kernel, n, window), out_shape=jax....]
where the time goes in v4:
time: 44.3 us; the launch traced here: 44.1 us
  Pallas kernels  40.6 us (92%)
  local copies, waits for them, and re-layouts  3.49 us (8%)
    pallas_call x1, Pallas kernels, fused_on_device(): pl.pallas_call(functools.partial(fused_kernel, n, window), out_shape=jax....  40.6 us
    reshape x1, local copies, waits for them, and re-layouts, fused_on_device(): bc = bc_input.reshape(rows, -1)  1.82 us
    unnamed x1, local copies, waits for them, and re-layouts  1.67 us

profile of v4, /device:TPU:0, one launch (start us, length us, event | category | flops | bytes accessed | tf_op | source)
XLA Modules:
  0.0 44.1 jit_solution(15938907020102894274)
XLA Ops:
  0.0 1.8 %reshape.6.bc_in = bf16[128,1024]{1,0:T(8,128)(2,1)} reshape(bf16[128,2,2,256]{3,2,1,0:T(2,128)(2,1)} %param.17) | data formatting | bytes 524288 | tf_op jit(solution)/shard_map/reshape | solution.py:723
  1.8 40.6 %shard_map.118 = bf16[128,1024]{1,0:T(8,128)(2,1)} custom-call(s32[4]{0:T(128)} %doc_ref.1, f32[16]{0:T(128)} %rate_ref.1, f32[16]{0:T(128)} %skip_ref.1, bf16[128,1024]{1,0:T(8,128)(2,1)} %q_in.1, bf16[128,128]{1,0:T(8,128)(2,1)} %k_in.1, bf16[128,128]{1,0:T(8,128)(2,1)} %v_in.1, bf16[128,1024]{1,0:T(8,128)(2,1)} %gate_in.1, ...), custom_call_target="tpu_custom_call" | custom-call | tf_op jit(solution)/shard_map/pallas_call | solution.py:730
  42.4 1.7 %copy.14 = bf16[128,1024]{1,0:T(8,128)(2,1)} copy(bf16[128,1024]{1,0:T(8,128)(2,1)} %shard_map.118) | data formatting | bytes 524288

commit v5 on v3

--- a/solution.py
+++ b/solution.py
@@ -525,42 +525,56 @@
             parts.append(jnp.where((key_pos <= pos) & (key_pos >= first), 0.0, NEGATIVE_FILL))
         return jnp.concatenate(parts, axis=1)
 
-    def attention(block, bias):
-        scores = dot_nt(block, keys) + bias
-        exponent = jnp.exp2((scores - jnp.max(scores, axis=1, keepdims=True)) * scale)
-        summed = dot_nn(exponent.astype(jnp.bfloat16), values)
-        return (summed[:, :LANES] / summed[:, LANES:]).astype(jnp.bfloat16).astype(jnp.float32)
+    def attention(blocks, biases):
+        scores = dot_nt(jnp.concatenate(blocks, axis=0), keys)
+        exponents = []
+        for j, bias in enumerate(biases):
+            part = scores[j * rows:(j + 1) * rows] + bias
+            exponents.append(jnp.exp2(
+                (part - jnp.max(part, axis=1, keepdims=True)) * scale).astype(jnp.bfloat16))
+        summed = dot_nn(jnp.concatenate(exponents, axis=0), values)
+        result = (summed[:, :LANES] / summed[:, LANES:]).astype(jnp.bfloat16).astype(jnp.float32)
+        return [result[j * rows:(j + 1) * rows] for j in range(len(blocks))]
 
     rim_block = jnp.concatenate(
         [q_rim[:, h * LANES:(h + 1) * LANES] for h in range(n)], axis=0)
     rim_pos = base - RIM + lax.rem(row_iota, RIM)
-    gated_ref[0] = attention(rim_block, bias_of(rim_pos))
+    rim_bias = bias_of(rim_pos)
     bias = bias_of(own_pos)
 
     def recv_bc(s):
         to_ctx(bc_all.at[s, core], bc_all.at[s, core], bc_send.at[0], bc_recv.at[s], pair).wait_recv()
 
     crossed = [pair] + [lax.rem(pair + 2 * k, n) for k in range(1, n // 2)]
-    for k in range(n):
-        h = lax.rem(me + 1 + k, n)
-        cols = pl.ds(pl.multiple_of(h * LANES, LANES), LANES)
-        attended = attention(q_ref[:, cols], bias)
-        rim = gated_ref[0, pl.ds(pl.multiple_of(h * RIM + RIM - 8, 8), 8), :]
-        x = conv(jnp.concatenate([rim, attended], axis=0), taps_ref[:, cols])
-        if k < n - 1:
-            x_out[h] = x
-            to_ctx(x_out.at[h], x_all.at[me], x_send.at[k], x_recv.at[me], h).start()
+    for part in range(2):
+        order = range(part * n // 2, (part + 1) * n // 2)
+        heads = [lax.rem(me + 1 + k, n) for k in order]
+        spans = [pl.ds(pl.multiple_of(h * LANES, LANES), LANES) for h in heads]
+        blocks = [q_ref[:, cols] for cols in spans]
+        if part == 0:
+            results = attention(blocks + [rim_block], [bias] * len(blocks) + [rim_bias])
+            gated_ref[0] = results.pop()
         else:
-            x_all[me] = x
-        if 1 <= k <= len(column):
-            s = column[k - 1]
-            recv_bc(s)
-            relay_bc(s, n // 2 + k - 1).start()
-            share_bc(s, k - 1).start()
-        if n // 2 <= k:
-            s = crossed[k - n // 2]
-            recv_bc(s)
-            share_bc(s, k - 1).start()
+            results = attention(blocks, [bias] * len(blocks))
+        outs = []
+        for h, cols, attended in zip(heads, spans, results):
+            rim = gated_ref[0, pl.ds(pl.multiple_of(h * RIM + RIM - 8, 8), 8), :]
+            outs.append(conv(jnp.concatenate([rim, attended], axis=0), taps_ref[:, cols]))
+        for k, h, x in zip(order, heads, outs):
+            if k < n - 1:
+                x_out[h] = x
+                to_ctx(x_out.at[h], x_all.at[me], x_send.at[k], x_recv.at[me], h).start()
+            else:
+                x_all[me] = x
+        if part == 0:
+            for k, s in enumerate(column):
+                recv_bc(s)
+                relay_bc(s, n // 2 + k).start()
+                share_bc(s, k).start()
+        else:
+            for k, s in enumerate(crossed):
+                recv_bc(s)
+                share_bc(s, n // 2 - 1 + k).start()
 
     upper = (row_iota <= lane_iota).astype(jnp.float32)
     left = lane_iota < LANES // 2

time: 43.3 us -> 42.7 us (0.986)
  Pallas kernels: 39.6 us -> 39 us
    pallas_call x1, Pallas kernels: 39.6 us -> 39 us  [fused_on_device(): pl.pallas_call(functools.partial(fused_kernel, n, window), out_shape=jax....]
where the time goes in v5:
time: 42.7 us; the launch traced here: 42.5 us
  Pallas kernels  39 us (91%)
  local copies, waits for them, and re-layouts  3.49 us (8%)
    pallas_call x1, Pallas kernels, fused_on_device(): pl.pallas_call(functools.partial(fused_kernel, n, window), out_shape=jax....  39 us
    reshape x1, local copies, waits for them, and re-layouts, fused_on_device(): bc = bc_input.reshape(rows, -1)  1.82 us
    unnamed x1, local copies, waits for them, and re-layouts  1.67 us

profile of v5, /device:TPU:0, one launch (start us, length us, event | category | flops | bytes accessed | tf_op | source)
XLA Modules:
  0.0 42.5 jit_solution(14025020113708797876)
XLA Ops:
  0.0 1.8 %reshape.6.bc_in = bf16[128,1024]{1,0:T(8,128)(2,1)} reshape(bf16[128,2,2,256]{3,2,1,0:T(2,128)(2,1)} %param.17) | data formatting | bytes 524288 | tf_op jit(solution)/shard_map/reshape | solution.py:703
  1.8 39.0 %shard_map.118 = bf16[128,1024]{1,0:T(8,128)(2,1)} custom-call(s32[4]{0:T(128)} %doc_ref.1, f32[16]{0:T(128)} %rate_ref.1, f32[16]{0:T(128)} %skip_ref.1, bf16[128,1024]{1,0:T(8,128)(2,1)} %q_in.1, bf16[128,128]{1,0:T(8,128)(2,1)} %k_in.1, bf16[128,128]{1,0:T(8,128)(2,1)} %v_in.1, bf16[128,1024]{1,0:T(8,128)(2,1)} %gate_in.1, ...), custom_call_target="tpu_custom_call" | custom-call | tf_op jit(solution)/shard_map/pallas_call | solution.py:709
  40.8 1.7 %copy.14 = bf16[128,1024]{1,0:T(8,128)(2,1)} copy(bf16[128,1024]{1,0:T(8,128)(2,1)} %shard_map.118) | data formatting | bytes 524288

commit v6 on v5

--- a/solution.py
+++ b/solution.py
@@ -483,6 +483,18 @@
         bc_own.append(to_ctx(bc_all.at[me, core], bc_all.at[me, core],
                              bc_send.at[1 + k], bc_recv.at[me], d))
 
+    def bias_of(pos):
+        first = first_of(pos)
+        parts = []
+        for r in range(window):
+            key_pos = (me - r) * rows + lane_iota
+            parts.append(jnp.where((key_pos <= pos) & (key_pos >= first), 0.0, NEGATIVE_FILL))
+        return jnp.concatenate(parts, axis=1)
+
+    rim_pos = base - RIM + lax.rem(row_iota, RIM)
+    rim_bias = bias_of(rim_pos)
+    bias = bias_of(own_pos)
+
     for r in range(2, window + 1, 2):
         cond = me >= r
         if r >= window:
@@ -516,14 +528,6 @@
     values = jnp.concatenate([kv[r, 1] for r in range(window)], axis=0)
     values = jnp.concatenate([values, jnp.ones_like(values)], axis=1)
     scale = math.log2(math.e) / math.sqrt(k_in.shape[1])
-
-    def bias_of(pos):
-        first = first_of(pos)
-        parts = []
-        for r in range(window):
-            key_pos = (me - r) * rows + lane_iota
-            parts.append(jnp.where((key_pos <= pos) & (key_pos >= first), 0.0, NEGATIVE_FILL))
-        return jnp.concatenate(parts, axis=1)
 
     def attention(blocks, biases):
         scores = dot_nt(jnp.concatenate(blocks, axis=0), keys)
@@ -538,9 +542,6 @@
 
     rim_block = jnp.concatenate(
         [q_rim[:, h * LANES:(h + 1) * LANES] for h in range(n)], axis=0)
-    rim_pos = base - RIM + lax.rem(row_iota, RIM)
-    rim_bias = bias_of(rim_pos)
-    bias = bias_of(own_pos)
 
     def recv_bc(s):
         to_ctx(bc_all.at[s, core], bc_all.at[s, core], bc_send.at[0], bc_recv.at[s], pair).wait_recv()

time: 42.7 us -> 42.6 us (level)
  no operation moved by 1% of the time
where the time goes in v6:
time: 42.6 us; the launch traced here: 42.4 us
  Pallas kernels  38.9 us (91%)
  local copies, waits for them, and re-layouts  3.49 us (8%)
    pallas_call x1, Pallas kernels, fused_on_device(): pl.pallas_call(functools.partial(fused_kernel, n, window), out_shape=jax....  38.9 us
    reshape x1, local copies, waits for them, and re-layouts, fused_on_device(): bc = bc_input.reshape(rows, -1)  1.82 us
    unnamed x1, local copies, waits for them, and re-layouts  1.67 us

profile of v6, /device:TPU:0, one launch (start us, length us, event | category | flops | bytes accessed | tf_op | source)
XLA Modules:
  0.0 42.4 jit_solution(9491108364910845560)
XLA Ops:
  0.0 1.8 %reshape.6.bc_in = bf16[128,1024]{1,0:T(8,128)(2,1)} reshape(bf16[128,2,2,256]{3,2,1,0:T(2,128)(2,1)} %param.17) | data formatting | bytes 524288 | tf_op jit(solution)/shard_map/reshape | solution.py:704
  1.8 38.9 %shard_map.118 = bf16[128,1024]{1,0:T(8,128)(2,1)} custom-call(s32[4]{0:T(128)} %doc_ref.1, f32[16]{0:T(128)} %rate_ref.1, f32[16]{0:T(128)} %skip_ref.1, bf16[128,1024]{1,0:T(8,128)(2,1)} %q_in.1, bf16[128,128]{1,0:T(8,128)(2,1)} %k_in.1, bf16[128,128]{1,0:T(8,128)(2,1)} %v_in.1, bf16[128,1024]{1,0:T(8,128)(2,1)} %gate_in.1, ...), custom_call_target="tpu_custom_call" | custom-call | tf_op jit(solution)/shard_map/pallas_call | solution.py:710
  40.8 1.7 %copy.14 = bf16[128,1024]{1,0:T(8,128)(2,1)} copy(bf16[128,1024]{1,0:T(8,128)(2,1)} %shard_map.118) | data formatting | bytes 524288
